TPU v7x, 32 devices: a whole 2x2x4 slice. The times are simulated.
32 devices in a mesh: dp: 16 (over z, x, core), tensor: 2 (over y).
Axes of the slice: x: 2, y: 2, z: 4, core: 2. Of those that a mesh axis runs over, the one named last changes fastest.
Arguments:
- inputs: bfloat16 [32768, 1024], P(('dp', 'tensor')), may hold values from -6 to 6
- attn_gain: bfloat16 [1024], P('dp'), may hold values from 0.5 to 1.5
- w_mix_in: bfloat16 [1024, 8, 768], P('dp', 'tensor'), may hold values from -0.1875 to 0.1875
- w_decay_beta: bfloat16 [1024, 8, 2], P('dp', 'tensor'), may hold values from -0.1875 to 0.1875
- conv_weight: float32 [4, 8, 512], P(None, 'tensor'), may hold values from -3 to 3
- a_log: float32 [8], P('tensor'), may hold values from -6 to 2.8
- dt_bias: float32 [8], P('tensor'), may hold values from -6.9 to -2.3
- head_gain: bfloat16 [256], P('dp'), may hold values from 0.5 to 1.5
- w_out: bfloat16 [8, 256, 1024], P('tensor', None, 'dp'), may hold values from -0.25 to 0.25
- mlp_gain: bfloat16 [1024], P('dp'), may hold values from 0.5 to 1.5
- w_gate_up: bfloat16 [1024, 2, 2816], P('dp', None, 'tensor'), may hold values from -0.1875 to 0.1875
- w_down: bfloat16 [2816, 1024], P('tensor', 'dp'), may hold values from -0.21875 to 0.21875
- cotangent: bfloat16 [32768, 1024], P(('dp', 'tensor')), may hold values from -6 to 6
Outputs:
- block_output: bfloat16 [32768, 1024], P(('dp', 'tensor'))
- input_grad: bfloat16 [32768, 1024], P(('dp', 'tensor'))
- attn_gain_grad: float32 [1024], P('dp')
- mix_in_grad: float32 [1024, 8, 768], P('dp', 'tensor')
- decay_beta_grad: float32 [1024, 8, 2], P('dp', 'tensor')
- conv_grad: float32 [4, 8, 512], P(None, 'tensor')
- a_log_grad: float32 [8], P('tensor')
- dt_bias_grad: float32 [8], P('tensor')
- head_gain_grad: float32 [256], P('dp')
- out_grad: float32 [8, 256, 1024], P('tensor', None, 'dp')
- mlp_gain_grad: float32 [1024], P('dp')
- gate_up_grad: float32 [1024, 2, 2816], P('dp', None, 'tensor')
- down_grad: float32 [2816, 1024], P('tensor', 'dp')
All inputs are finite; a program needn't handle non-finite values.
Results may differ from a plain program's by a relative error of at most 0.02.
Values may be sent and summed in bfloat16 or wider, within the bound.
A program may use at most 512 MiB of HBM per device.

v0:
```python
import jax
import jax.numpy as jnp
from jax import lax
from jax.sharding import PartitionSpec as P

DK = 128
DV = 256
CONV = 4
LEN = 2048
BLOCK = 64


EPSILON = 1e-06
highest = lax.Precision.HIGHEST


def rms_scale(rows):
    return rows * lax.rsqrt(jnp.mean(rows * rows, axis=-1, keepdims=True) + EPSILON)


def unit_rows(rows):
    return rows * lax.rsqrt(jnp.sum(rows * rows, axis=-1, keepdims=True) + EPSILON)


def rms_back(rows, gain, grad):
    scale = lax.rsqrt(jnp.mean(rows * rows, axis=-1, keepdims=True) + EPSILON)
    normed = rows * scale
    weighted = grad * gain
    back = scale * (weighted - normed * jnp.mean(weighted * normed, axis=-1, keepdims=True))
    return (back, jnp.sum(grad * normed, axis=0))


def matmul(left, right):
    return jnp.dot(left, right, preferred_element_type=jnp.float32)


def contract_rows(left, right):
    return lax.dot_general(
        left, right, (((0,), (0,)), ((), ())), preferred_element_type=jnp.float32
    )


def contract_last(left, right):
    return lax.dot_general(
        left, right, (((1,), (1,)), ((), ())), preferred_element_type=jnp.float32
    )


def delta_rule(queries, keys, values, beta, logdecay):
    size = keys.shape[2]
    key_width = keys.shape[3]
    cumulative = jnp.cumsum(logdecay, axis=2)
    order = jnp.arange(size)
    strict = order[:, None] > order[None, :]
    inclusive = order[:, None] >= order[None, :]
    spread = cumulative[:, :, :, None] - cumulative[:, :, None, :]
    below = jnp.where(strict, jnp.exp(jnp.where(strict, spread, 0.0)), 0.0)
    within = jnp.where(inclusive, jnp.exp(jnp.where(inclusive, spread, 0.0)), 0.0)
    decay_now = jnp.exp(cumulative)
    decay_tail = jnp.exp(cumulative[:, :, -1:] - cumulative)
    key_dots = jnp.einsum("bnck,bnjk->bncj", keys, keys, precision=highest)
    system = jnp.eye(size, dtype=jnp.float32) + beta[:, :, :, None] * key_dots * below
    right = jnp.concatenate(
        [(beta * decay_now)[..., None] * keys, beta[..., None] * values], axis=-1
    )
    solved = jax.scipy.linalg.solve_triangular(system, right, lower=True, unit_diagonal=True)
    weights_w = solved[..., :key_width]
    fresh = solved[..., key_width:]
    tail_keys = decay_tail[..., None] * keys
    block_decay = decay_now[:, :, -1]

    def advance(state, pieces):
        piece_w, piece_fresh, piece_keys, piece_decay = pieces
        updates = piece_fresh - jnp.einsum("bck,bkv->bcv", piece_w, state, precision=highest)
        following = piece_decay[:, None, None] * state + jnp.einsum(
            "bck,bcv->bkv", piece_keys, updates, precision=highest
        )
        return (following, (state, updates))

    start = jnp.zeros((keys.shape[0], key_width, values.shape[3]), jnp.float32)
    moved = tuple(
        (jnp.moveaxis(array, 1, 0) for array in (weights_w, fresh, tail_keys, block_decay))
    )
    ending, (states, updates) = lax.scan(advance, start, moved)
    states = jnp.moveaxis(states, 0, 1)
    updates = jnp.moveaxis(updates, 0, 1)
    query_dots = jnp.einsum("bnck,bnjk->bncj", queries, keys, precision=highest) * within
    carried = jnp.einsum(
        "bnck,bnkv->bncv", decay_now[..., None] * queries, states, precision=highest
    )
    return carried + jnp.einsum("bncj,bnjv->bncv", query_dots, updates, precision=highest)


def mix_core(mixed_in, small, conv_weight, a_log, dt_bias, head_gain):
    count, heads, columns = mixed_in.shape
    conv_width = conv_weight.shape[2]
    seqs = count // LEN
    conv_in = mixed_in[:, :, :conv_width].reshape(seqs, LEN, heads * conv_width)
    kernel = conv_weight.reshape(CONV, heads * conv_width)
    padded = jnp.pad(conv_in, ((0, 0), (CONV - 1, 0), (0, 0)))
    mixed = padded[:, 0:LEN] * kernel[0]
    for offset in range(1, CONV):
        mixed = mixed + padded[:, offset : offset + LEN] * kernel[offset]
    active = jax.nn.silu(mixed).reshape(count, heads, conv_width)
    queries = unit_rows(active[:, :, :DK]) * DK ** (-0.5)
    keys = unit_rows(active[:, :, DK : 2 * DK])
    values = active[:, :, 2 * DK :]
    beta = jax.nn.sigmoid(small[:, :, 1])
    logdecay = -jnp.exp(a_log) * jax.nn.softplus(small[:, :, 0] + dt_bias)

    def blocks(array):
        rest = array.shape[2:]
        shaped = array.reshape((seqs, LEN // BLOCK, BLOCK, heads) + rest)
        moved = jnp.moveaxis(shaped, 3, 1)
        return moved.reshape((seqs * heads, LEN // BLOCK, BLOCK) + rest)

    outputs = delta_rule(
        blocks(queries), blocks(keys), blocks(values), blocks(beta), blocks(logdecay)
    )
    outputs = jnp.moveaxis(outputs.reshape(seqs, heads, LEN, DV), 1, 2).reshape(count, heads, DV)
    gate = mixed_in[:, :, conv_width:]
    return rms_scale(outputs) * head_gain * jax.nn.silu(gate)


def gather_rows(piece):
    return lax.all_gather(piece, "tensor", axis=0, tiled=True)


def row_sums(partial_value):
    return lax.psum_scatter(partial_value, "tensor", scatter_dimension=0, tiled=True)


def per_device(
    inputs,
    attn_gain,
    w_mix_in,
    w_decay_beta,
    conv_weight,
    a_log,
    dt_bias,
    head_gain,
    w_out,
    mlp_gain,
    w_gate_up,
    w_down,
    cotangent,
):
    mix_full, small_full, out_full, attn_full, head_full = (
        lax.all_gather(w_mix_in, "dp", axis=0, tiled=True),
        lax.all_gather(w_decay_beta, "dp", axis=0, tiled=True),
        lax.all_gather(w_out, "dp", axis=2, tiled=True),
        lax.all_gather(attn_gain, "dp", axis=0, tiled=True),
        lax.all_gather(head_gain, "dp", axis=0, tiled=True),
    )
    width = mix_full.shape[0]
    heads = mix_full.shape[1]
    residual = inputs.astype(jnp.float32)
    attn_scale = attn_full.astype(jnp.float32)
    piece_one = (rms_scale(residual) * attn_scale).astype(jnp.bfloat16)
    normed_one = gather_rows(piece_one)
    count = normed_one.shape[0]
    mix_matrix = mix_full.reshape(width, -1)
    small_matrix = small_full.reshape(width, -1)
    mixed_in = matmul(normed_one, mix_matrix).reshape(count, heads, -1)
    small = matmul(normed_one, small_matrix).reshape(count, heads, 2)
    gated, core_back = jax.vjp(
        mix_core, mixed_in, small, conv_weight, a_log, dt_bias, head_full.astype(jnp.float32)
    )
    gated_low = gated.astype(jnp.bfloat16).reshape(count, -1)
    out_matrix = out_full.reshape(-1, width)
    middle = residual + row_sums(matmul(gated_low, out_matrix))
    gate_up_full, down_full, mlp_full = (
        lax.all_gather(w_gate_up, "dp", axis=0, tiled=True),
        lax.all_gather(w_down, "dp", axis=1, tiled=True),
        lax.all_gather(mlp_gain, "dp", axis=0, tiled=True),
    )
    mlp_scale = mlp_full.astype(jnp.float32)
    piece_two = (rms_scale(middle) * mlp_scale).astype(jnp.bfloat16)
    normed_two = gather_rows(piece_two)
    units = gate_up_full.shape[2]
    gate_up_matrix = gate_up_full.reshape(width, 2 * units)
    both = matmul(normed_two, gate_up_matrix)
    gate = both[:, :units]
    up = both[:, units:]
    hidden = (jax.nn.silu(gate) * up).astype(jnp.bfloat16)
    block_output = (middle + row_sums(matmul(hidden, down_full))).astype(jnp.bfloat16)
    back_rows = gather_rows(cotangent)
    d_hidden = contract_last(back_rows, down_full)
    sigmoid_gate = jax.nn.sigmoid(gate)
    d_gate = d_hidden * up * sigmoid_gate * (1.0 + gate * (1.0 - sigmoid_gate))
    d_up = d_hidden * gate * sigmoid_gate
    d_both = jnp.concatenate([d_gate, d_up], axis=1).astype(jnp.bfloat16)
    grad_down = contract_rows(hidden, back_rows)
    grad_gate_up = contract_rows(normed_two, d_both).reshape(width, 2, units)
    d_normed_two = row_sums(contract_last(d_both, gate_up_matrix))
    d_middle, grad_mlp_gain = rms_back(middle, mlp_scale, d_normed_two)
    d_middle = d_middle + cotangent.astype(jnp.float32)
    middle_rows = gather_rows(d_middle.astype(jnp.bfloat16))
    grad_out = contract_rows(gated_low, middle_rows).reshape(heads, -1, width)
    d_gated = contract_last(middle_rows, out_matrix).reshape(count, heads, -1)
    d_mixed, d_small, d_conv, d_decay_log, d_bias, d_head = core_back(d_gated)
    d_mixed_low = d_mixed.reshape(count, -1).astype(jnp.bfloat16)
    d_small_low = d_small.reshape(count, -1).astype(jnp.bfloat16)
    grad_mix_in = contract_rows(normed_one, d_mixed_low).reshape(width, heads, -1)
    grad_decay_beta = contract_rows(normed_one, d_small_low).reshape(width, heads, 2)
    d_normed_one = row_sums(
        contract_last(d_mixed_low, mix_matrix) + contract_last(d_small_low, small_matrix)
    )
    d_inputs, grad_attn_gain = rms_back(residual, attn_scale, d_normed_one)
    input_grad = (d_inputs + d_middle).astype(jnp.bfloat16)
    every_sum = (
        lax.psum_scatter(
            grad_gate_up.astype(jnp.bfloat16), "dp", scatter_dimension=0, tiled=True
        ).astype(jnp.float32),
        lax.psum_scatter(
            grad_down.astype(jnp.bfloat16), "dp", scatter_dimension=1, tiled=True
        ).astype(jnp.float32),
        lax.psum_scatter(
            grad_mlp_gain.astype(jnp.bfloat16), "dp", scatter_dimension=0, tiled=True
        ).astype(jnp.float32),
        lax.psum_scatter(
            grad_mix_in.astype(jnp.bfloat16), "dp", scatter_dimension=0, tiled=True
        ).astype(jnp.float32),
        lax.psum_scatter(
            grad_decay_beta.astype(jnp.bfloat16), "dp", scatter_dimension=0, tiled=True
        ).astype(jnp.float32),
        lax.psum_scatter(
            grad_out.astype(jnp.bfloat16), "dp", scatter_dimension=2, tiled=True
        ).astype(jnp.float32),
        lax.psum_scatter(
            grad_attn_gain.astype(jnp.bfloat16), "dp", scatter_dimension=0, tiled=True
        ).astype(jnp.float32),
        lax.psum_scatter(d_head.astype(jnp.bfloat16), "dp", scatter_dimension=0, tiled=True).astype(
            jnp.float32
        ),
    )
    mlp_sums = every_sum[:3]
    mixer_sums = every_sum[3:]
    gain_attn, gain_head, gain_mlp = lax.psum((mixer_sums[3], mixer_sums[4], mlp_sums[2]), "tensor")
    conv_total, decay_total, bias_total = lax.psum((d_conv, d_decay_log, d_bias), "dp")
    return (
        block_output,
        input_grad,
        gain_attn,
        mixer_sums[0],
        mixer_sums[1],
        conv_total,
        decay_total,
        bias_total,
        gain_head,
        mixer_sums[2],
        gain_mlp,
        mlp_sums[0],
        mlp_sums[1],
    )


def solution(mesh):
    in_specs = (
        P(("dp", "tensor"), None),
        P("dp"),
        P("dp", "tensor", None),
        P("dp", "tensor", None),
        P(None, "tensor", None),
        P("tensor"),
        P("tensor"),
        P("dp"),
        P("tensor", None, "dp"),
        P("dp"),
        P("dp", None, "tensor"),
        P("tensor", "dp"),
        P(("dp", "tensor"), None),
    )
    out_specs = (
        P(("dp", "tensor"), None),
        P(("dp", "tensor"), None),
        P("dp"),
        P("dp", "tensor", None),
        P("dp", "tensor", None),
        P(None, "tensor", None),
        P("tensor"),
        P("tensor"),
        P("dp"),
        P("tensor", None, "dp"),
        P("dp"),
        P("dp", None, "tensor"),
        P("tensor", "dp"),
    )
    return jax.shard_map(
        per_device, mesh=mesh, in_specs=in_specs, out_specs=out_specs, check_vma=False
    )
```

profile of v0, /device:TPU:0, one launch (start us, length us, event | category | flops | bytes accessed | tf_op | source)
XLA Modules:
  0.0 2596.4 jit_solution(6155610083222105377)
XLA Ops:
  12.4 36.0 %all-reduce.30 = (bf16[1024]{0:T(1024)(128)(2,1)S(1)}, bf16[256]{0:T(256)(128)(2,1)S(1)}, bf16[1024]{0:T(1024)(128)(2,1)}) all-reduce(bf16[1024]{0:T(1024)(128)(2,1)S(1)} %dynamic-update-slice, bf16[256]{0:T(256)(128)(2,1)S(1)} %dynamic-update-slice.1, bf16[1024]{0:T(1024)(128)(2,1)S(1)} %dynamic-update-slice.2), channel_id=1, replica_groups=mesh['dp'=16,'tensor'=2] {'dp'}, use_global_device_ids=true, to_apply=%add.20 | all-reduce | flops 2304 | bytes 9216
  56.5 18.9 all_gather.38
  76.6 32.2 %all-gather.9.cloned.1.call-done = bf16[2048,1024]{1,0:T(8,128)(2,1)} async-done(((bf16[1024,1024]{1,0:T(8,128)(2,1)}), bf16[2048,1024]{1,0:T(8,128)(2,1)}) %all-gather.9.cloned.1.call-update) | async-done | bytes 4194320 | tf_op jit(solution)/shard_map/all_gather | solution.py:126
  114.9 58.8 %all-gather.11.cloned.1.call-done = bf16[1024,4,768]{2,0,1:T(8,128)(2,1)} async-done(((bf16[64,4,768]{2,0,1:T(8,128)(2,1)}), bf16[1024,4,768]{2,0,1:T(8,128)(2,1)}) %all-gather.11.cloned.1.call-update) | async-done | bytes 6291472 | tf_op jit(solution)/shard_map/all_gather | solution.py:149
  173.7 8.7 copy.212
  182.3 16.5 fusion.88
  212.5 38.7 %fusion.39 = (f32[1,2048,2048]{1,2,0:T(8,128)}, f32[1,2048,2048]{1,2,0:T(8,128)}) fusion(f32[1,2048,2048]{1,2,0:T(8,128)} %bitcast.383, f32[2048]{0:T(1024)S(1)} %bitcast.423, f32[2048]{0:T(1024)S(1)} %bitcast.421, f32[2048]{0:T(1024)S(1)} %bitcast.419, f32[2048]{0:T(1024)S(1)} %bitcast.417), kind=kLoop, calls=%fused_computation.66 | loop fusion | flops 46137344 | bytes 50364416 | tf_op jit(solution)/shard_map/jvp(jit(silu))/mul | solution.py:104
  251.2 8.8 fusion.167
  283.9 8.5 broadcast_multiply_fusion.5
  292.4 8.2 fusion.169
  315.9 9.2 copy.216
  325.1 12.8 fusion.69
  337.9 265.4 %custom-call.10 = f32[4,32,1,64,64]{1,3,4,2,0:T(8,128)} custom-call(f32[4,32,1,64,64]{1,4,3,2,0:T(8,128)} %get-tuple-element.645), custom_call_target="InvertDiagBlocksLowerTriangular" | custom-call | tf_op jit(solution)/shard_map/jvp(jit(_solve_triangular))/vmap(vmap())/triangular_solve | solution.py:66
  603.3 8.7 copy.220
  612.1 8.7 copy.291
  629.6 14.6 fusion.44
  666.1 166.6 %while.40 = (s32[]{:T(128)}, f32[4,128,256]{2,1,0:T(8,128)S(1)}, f32[32,4,128,256]{3,2,1,0:T(8,128)}, f32[32,4,64,256]{3,2,1,0:T(8,128)}, f32[32,4,1,1]{1,3,2,0:...) while((s32[]{:T(128)}, f32[4,128,256]{2,1,0:T(8,128)S(1)}, ...), condition=%wide.region_5.6_spmd.clone, body=%wide.region_4.5_spmd.clone.sunk | while | flops 202047488 | bytes 3935421 | solution.py:84
  839.9 16.4 fusion.42
  856.4 12.5 fusion.129
  868.9 8.7 copy.229
  890.0 10.7 convolution_bitcast_fusion.2
  901.4 97.7 %reduce-scatter.11.cloned.1.call-done = f32[1024,1024]{1,0:T(8,128)} async-done(((f32[2048,1024]{1,0:T(8,128)}), f32[1024,1024]{1,0:T(8,128)}) %reduce-scatter.11.cloned.1.call-update) | async-done | bytes 4194320 | tf_op jit(solution)/shard_map/reduce_scatter | solution.py:130
  1007.2 53.3 %all-gather.17.cloned.1.call-done = bf16[1024,2,1408]{2,1,0:T(2,128)(2,1)} async-done(((bf16[64,2,1408]{2,1,0:T(2,128)(2,1)}), bf16[1024,2,1408]{2,1,0:T(2,128)(2,1)}) %all-gather.17.cloned.1.call-update) | async-done | bytes 5767184 | tf_op jit(solution)/shard_map/all_gather | solution.py:173
  1066.7 51.3 %all-gather.15.cloned.1.call-done = bf16[2048,1024]{1,0:T(8,128)(2,1)} async-done(((bf16[1024,1024]{1,0:T(8,128)(2,1)}), bf16[2048,1024]{1,0:T(8,128)(2,1)}) %all-gather.15.cloned.1.call-update) | async-done | bytes 4194320 | tf_op jit(solution)/shard_map/all_gather | solution.py:126
  1118.0 20.2 fusion.171
  1138.2 38.2 %all-gather.21.cloned.1.call-done = bf16[2048,1024]{1,0:T(8,128)(2,1)} async-done(((bf16[1024,1024]{1,0:T(8,128)(2,1)}), bf16[2048,1024]{1,0:T(8,128)(2,1)}) %all-gather.21.cloned.1.call-update) | async-done | bytes 4194320 | tf_op jit(solution)/shard_map/all_gather | solution.py:126
  1176.4 46.9 %all-gather.19.cloned.1.call-done = bf16[1408,1024]{0,1:T(8,128)(2,1)} async-done(((bf16[1408,64]{0,1:T(8,128)(2,1)}), bf16[1408,1024]{0,1:T(8,128)(2,1)}) %all-gather.19.cloned.1.call-update) | async-done | bytes 2883600 | tf_op jit(solution)/shard_map/all_gather | solution.py:174
  1223.3 21.5 multiply_convert_fusion.1
  1244.8 17.9 fusion.87
  1263.0 97.5 %reduce-scatter.15.cloned.1.call-done = f32[1024,1024]{1,0:T(8,128)} async-done(((f32[2048,1024]{1,0:T(8,128)}), f32[1024,1024]{1,0:T(8,128)}) %reduce-scatter.15.cloned.1.call-update) | async-done | bytes 4194320 | tf_op jit(solution)/shard_map/reduce_scatter | solution.py:130
  1368.9 19.0 fusion.94
  1387.8 12.1 convert_element_type.141
  1400.2 8.7 copy.238
  1416.3 11.5 convolution_convert_fusion
  1428.1 18.5 multiply_reduce_fusion.4
  1446.7 14.3 fusion.73
  1461.0 8.8 copy.235
  1469.8 21.0 fusion.80
  1490.8 16.1 fusion.82
  1506.9 24.5 multiply_reduce_fusion.9
  1531.3 15.7 fusion.78
  1556.5 337.3 %while.41 = (s32[]{:T(128)}, f32[4,128,256]{2,1,0:T(8,128)S(1)}, f32[32,4,64,128]{3,2,1,0:T(8,128)}, f32[32,4,64,256]{3,2,1,0:T(8,128)}, f32[32,4,64,128]{3,2,0,...) while((s32[]{:T(128)}, f32[4,128,256]{2,1,0:T(8,128)S(1)}, ...), condition=%wide.region_15.16_spmd.clone, body=%wide.region_13.15_spmd.clone.sunk | while | flops 404029440 | bytes 6297367 | solution.py:84
  1893.8 20.4 fusion.50
  1919.7 9.2 copy.251
  1935.9 25.1 fusion.64
  1968.2 12.2 fusion.173
  1988.1 12.4 fusion.175
  2000.5 15.5 fusion.52
  2020.7 9.8 fusion.112
  2038.6 8.4 multiply_add_fusion.1
  2067.9 16.5 copy.256
  2092.4 45.2 %multiply_reduce_fusion.2 = (f32[2048]{0:T(1024)}, f32[2048]{0:T(1024)}, f32[2048]{0:T(1024)}, f32[2048]{0:T(1024)}, f32[1,2048,2048]{1,2,0:T(8,128)}) fusion(f32[1,2048,2048]{1,2,0:T(8,128)} %bitcast.384, f32[2048,4,512]{0,2,1:T(8,128)} %slice.105, f32[1,2048,2048]{1,2,0:T(8,128)} %get-tuple-element.619, f32[2048,4,512]{0,2,1:T(8,128)} %copy.256), kind=kLoop, calls=%fused_computation.62 | loop fusion | flops 71294976 | bytes 83918848 | tf_op jit(solution)/shard_map/transpose(jvp())/reduce_sum | solution.py:103
  2142.2 26.7 %broadcast_multiply_fusion = (f32[1,2048,2048]{1,2,0:T(8,128)}, f32[1,2048,2048]{1,2,0:T(8,128)}, f32[1,2048,2048]{1,2,0:T(8,128)}, f32[1,2048,2048]{1,2,0:T(8,128)}) fusion(f32[1,2048,2048]{1,2,0:T(8,128)} %get-tuple-element.611, f32[2048]{0:T(1024)S(1)} %bitcast.424, f32[2048]{0:T(1024)S(1)} %bitcast.418, f32[2048]{0:T(1024)S(1)} %bitcast.420, ...), kind=kLoop, calls=%fused_computation.130 | loop fusion | flops 16777216 | bytes 83918848 | tf_op jit(solution)/shard_map/transpose(jvp())/mul | solution.py:103
  2169.4 9.3 fusion.132
  2178.8 29.9 %pad_add_fusion = f32[1,2048,2048]{1,2,0:T(8,128)} fusion(f32[1,2048,2048]{1,2,0:T(8,128)} %get-tuple-element.631, f32[1,2048,2048]{1,2,0:T(8,128)} %get-tuple-element.632, f32[1,2048,2048]{1,2,0:T(8,128)} %get-tuple-element.633, f32[1,2048,2048]{1,2,0:T(8,128)} %get-tuple-element.630), kind=kLoop, calls=%fused_computation.55 | loop fusion | flops 12582912 | bytes 83886080 | tf_op jit(solution)/shard_map/transpose(jvp())/add_any | solution.py:101
  2208.8 19.8 fusion.124
  2233.8 22.0 bitcast_add_fusion.1
  2257.6 10.7 fusion.172
  2274.2 62.8 %all-reduce.27 = (f32[4,4,512]{2,1,0:T(4,128)}, f32[4]{0:T(128)}, f32[4]{0:T(128)}) all-reduce(f32[4,4,512]{2,1,0:T(4,128)S(1)} %reshape.572, f32[4]{0:T(128)S(1)} %negate_multiply_fusion, f32[4]{0:T(128)S(1)} %get-tuple-element.553), channel_id=1, replica_groups=mesh['dp'=16,'tensor'=2] {'dp'}, use_global_device_ids=true, to_apply=%region_38.39 | all-reduce | flops 8200 | bytes 65600 | tf_op jit(solution)/shard_map/psum | solution.py:240
  2340.1 37.6 %reduce-scatter.19.cloned.1.call-done = bf16[64,4,768]{2,0,1:T(8,128)(2,1)} async-done(((bf16[1024,4,768]{2,0,1:T(8,128)(2,1)}), bf16[64,4,768]{2,0,1:T(8,128)(2,1)}) %reduce-scatter.19.cloned.1.call-update) | async-done | bytes 393232 | tf_op jit(solution)/shard_map/reduce_scatter | solution.py:221
  2379.9 98.6 %reduce-scatter.17.cloned.1.call-done = f32[1024,1024]{1,0:T(8,128)} async-done(((f32[2048,1024]{1,0:T(8,128)}), f32[1024,1024]{1,0:T(8,128)}) %reduce-scatter.17.cloned.1.call-update) | async-done | bytes 4194320 | tf_op jit(solution)/shard_map/reduce_scatter | solution.py:130
  2481.9 33.7 %all-reduce.29 = (bf16[1024]{0:T(1024)(128)(2,1)S(1)}, bf16[256]{0:T(256)(128)(2,1)S(1)}, bf16[1024]{0:T(1024)(128)(2,1)S(1)}) all-reduce(bf16[1024]{0:T(1024)(128)(2,1)S(1)} %get-tuple-element.549, bf16[256]{0:T(256)(128)(2,1)S(1)} %copy-done.103, bf16[1024]{0:T(1024)(128)(2,1)S(1)} %copy-done.92), channel_id=6, replica_groups=mesh['dp'=16,'tensor'=2] {'dp'}, use_global_device_ids=true, to_apply=%region_30.31.clone | all-reduce | flops 2304 | bytes 9216
  2521.2 58.7 %reduce-scatter.13.cloned.1.call-done = f32[1024,1024]{1,0:T(8,128)} async-done(((f32[2048,1024]{1,0:T(8,128)}), f32[1024,1024]{1,0:T(8,128)}) %reduce-scatter.13.cloned.1.call-update) | async-done | bytes 4194320 | tf_op jit(solution)/shard_map/reduce_scatter | solution.py:130
  2580.0 9.7 fusion.101
  (774 shorter events, 765.2 us)
Async XLA Ops:
  7.2 47.5 %copy-start.50 = (bf16[64,4,768]{2,1,0:T(4,128)(2,1)S(1)}, bf16[64,4,768]{2,1,0:T(4,128)(2,1)}, u32[]{:S(2)}) copy-start(bf16[64,4,768]{2,1,0:T(4,128)(2,1)} %param.19) | copy-start | bytes 1179652
  7.2 49.2 %copy-start.101 = (bf16[64,4,2]{0,2,1:T(2,128)(2,1)S(1)}, bf16[64,4,2]{0,2,1:T(2,128)(2,1)}, u32[]{:S(2)}) copy-start(bf16[64,4,2]{0,2,1:T(2,128)(2,1)} %param.20) | copy-start | bytes 3076
  7.2 68.6 %copy-start.106 = (f32[4]{0:T(128)S(1)}, f32[4]{0:T(128)}, u32[]{:S(2)}) copy-start(f32[4]{0:T(128)} %param.22) | copy-start | bytes 52
  7.2 68.6 %copy-start.91 = (f32[4,4,512]{2,1,0:T(4,128)S(1)}, f32[4,4,512]{2,1,0:T(4,128)}, u32[]{:S(2)}) copy-start(f32[4,4,512]{2,1,0:T(4,128)} %param.21) | copy-start | bytes 98308
  7.2 101.6 %all-gather.9.cloned.1.call-start = ((), (), s32[]{:S(2)}) async-start(), calls=%async_computation.8 | async-start | bytes 6291456 | tf_op jit(solution)/shard_map/all_gather | solution.py:126
  48.4 64.5 %copy-start.93 = (f32[4]{0:T(128)S(1)}, f32[4]{0:T(128)}, u32[]{:S(2)}) copy-start(f32[4]{0:T(128)} %param.23) | copy-start | bytes 52
  54.6 119.1 %all-gather.11.cloned.1.call-start = ((), (), s32[]{:S(2)}) async-start(), calls=%async_computation.9 | async-start | bytes 6684672 | tf_op jit(solution)/shard_map/all_gather | solution.py:149
  55.5 834.5 %all-gather.13.cloned.1.call-start = ((), (), s32[]{:S(2)}) async-start(), calls=%async_computation.10 | async-start | bytes 2228224 | tf_op jit(solution)/shard_map/all_gather | solution.py:151
  56.2 942.9 %reduce-scatter.11.cloned.1.call-start = ((), (), s32[]{:S(2)}) async-start(), calls=%async_computation.11 | async-start | bytes 12582912 | tf_op jit(solution)/shard_map/reduce_scatter | solution.py:130
  56.3 268.8 %copy-start.67 = (pred[64,64]{1,0:T(8,128)(4,1)}, pred[64,64]{1,0:T(8,128)(4,1)S(1)}, u32[]{:S(2)}) copy-start(pred[64,64]{1,0:T(8,128)(4,1)S(1)} %get-tuple-element.664) | copy-start | bytes 12292
  56.3 268.7 %copy-start.69 = (pred[64,64]{1,0:T(8,128)(4,1)}, pred[64,64]{1,0:T(8,128)(4,1)S(1)}, u32[]{:S(2)}) copy-start(pred[64,64]{1,0:T(8,128)(4,1)S(1)} %get-tuple-element.665) | copy-start | bytes 12292
  75.3 107.0 %copy-start.28 = (bf16[1024,4,2]{1,2,0:T(2,128)(2,1)}, bf16[1024,4,2]{1,2,0:T(2,128)(2,1)S(1)}, u32[]{:S(2)}) copy-start(bf16[1024,4,2]{1,2,0:T(2,128)(2,1)S(1)} %all_gather.38) | copy-start | bytes 49156
  75.8 38.4 %copy-start.96 = (f32[4]{0:T(128)}, f32[4]{0:T(128)S(1)}, u32[]{:S(2)}) copy-start(f32[4]{0:T(128)S(1)} %exponential_negate_fusion) | copy-start | bytes 52
  75.8 136.6 %copy-start.73 = (f32[1,4,4,128]{3,1,2,0:T(4,128)}, f32[1,4,4,128]{3,1,2,0:T(4,128)S(1)}, u32[]{:S(2)}) copy-start(f32[1,4,4,128]{3,1,2,0:T(4,128)S(1)} %copy.342) | copy-start | bytes 24580
  75.9 136.6 %copy-start.75 = (f32[1,4,4,128]{3,1,2,0:T(4,128)}, f32[1,4,4,128]{3,1,2,0:T(4,128)S(1)}, u32[]{:S(2)}) copy-start(f32[1,4,4,128]{3,1,2,0:T(4,128)S(1)} %copy.343) | copy-start | bytes 24580
  75.9 136.6 %copy-start.77 = (f32[1,4,4,128]{3,1,2,0:T(4,128)}, f32[1,4,4,128]{3,1,2,0:T(4,128)S(1)}, u32[]{:S(2)}) copy-start(f32[1,4,4,128]{3,1,2,0:T(4,128)S(1)} %copy.344) | copy-start | bytes 24580
  75.9 136.6 %copy-start.79 = (f32[1,4,4,128]{3,1,2,0:T(4,128)}, f32[1,4,4,128]{3,1,2,0:T(4,128)S(1)}, u32[]{:S(2)}) copy-start(f32[1,4,4,128]{3,1,2,0:T(4,128)S(1)} %copy.345) | copy-start | bytes 24580
  76.0 249.0 %copy-start.71 = (pred[64,64]{1,0:T(8,128)(4,1)}, pred[64,64]{1,0:T(8,128)(4,1)S(1)}, u32[]{:S(2)}) copy-start(pred[64,64]{1,0:T(8,128)(4,1)S(1)} %get-tuple-element.666) | copy-start | bytes 12292
  113.9 84.9 %copy-start.36 = (f32[4,32,64]{2,1,0:T(8,128)}, f32[4,32,64]{2,1,0:T(8,128)S(1)}, u32[]{:S(2)}) copy-start(f32[4,32,64]{2,1,0:T(8,128)S(1)} %reduce_window_sum.24) | copy-start | bytes 98308
  114.2 210.8 %copy-start.30 = (f32[4,32,64]{1,2,0:T(8,128)}, f32[4,32,64]{1,2,0:T(8,128)S(1)}, u32[]{:S(2)}) copy-start(f32[4,32,64]{1,2,0:T(8,128)S(1)} %copy.217) | copy-start | bytes 98308
  114.3 506.4 %copy-start.32 = (f32[1,32,64,4]{2,1,3,0:T(8,128)}, f32[1,32,64,4]{2,1,3,0:T(8,128)S(1)}, u32[]{:S(2)}) copy-start(f32[1,32,64,4]{2,1,3,0:T(8,128)S(1)} %div.68) | copy-start | bytes 98308
  114.4 169.5 %copy-start.40 = (f32[4,32,64]{2,1,0:T(8,128)}, f32[4,32,64]{2,1,0:T(8,128)S(1)}, u32[]{:S(2)}) copy-start(f32[4,32,64]{2,1,0:T(8,128)S(1)} %get-tuple-element.648) | copy-start | bytes 98308
  114.5 169.5 %copy-start.42 = (f32[4,32,64]{2,1,0:T(8,128)}, f32[4,32,64]{2,1,0:T(8,128)S(1)}, u32[]{:S(2)}) copy-start(f32[4,32,64]{2,1,0:T(8,128)S(1)} %get-tuple-element.646) | copy-start | bytes 98308
  114.5 542.5 %copy-start.34 = (f32[4,32,64]{2,1,0:T(8,128)}, f32[4,32,64]{2,1,0:T(8,128)S(1)}, u32[]{:S(2)}) copy-start(f32[4,32,64]{2,1,0:T(8,128)S(1)} %get-tuple-element.647) | copy-start | bytes 98308
  114.6 210.5 %copy-start.38 = (f32[4,32,64]{1,2,0:T(8,128)}, f32[4,32,64]{1,2,0:T(8,128)S(1)}, u32[]{:S(2)}) copy-start(f32[4,32,64]{1,2,0:T(8,128)S(1)} %copy.215) | copy-start | bytes 98308
  275.1 17.3 copy-start.55
  900.7 98.4 %copy-start.12 = (bf16[1024,1024]{1,0:T(8,128)(2,1)S(1)}, bf16[1024,1024]{1,0:T(8,128)(2,1)}, u32[]{:S(2)}) copy-start(bf16[1024,1024]{1,0:T(8,128)(2,1)} %param.17) | copy-start | bytes 6291460
  900.7 159.8 %all-gather.17.cloned.1.call-start = ((), (), s32[]{:S(2)}) async-start(), calls=%async_computation.13 | async-start | bytes 6127616 | tf_op jit(solution)/shard_map/all_gather | solution.py:173
  901.3 216.7 %all-gather.15.cloned.1.call-start = ((), (), s32[]{:S(2)}) async-start(), calls=%async_computation.12 | async-start | bytes 6291456 | tf_op jit(solution)/shard_map/all_gather | solution.py:126
  901.4 464.4 %copy-start.63 = (f32[1024]{0:T(1024)}, f32[1024]{0:T(1024)S(1)}, u32[]{:S(2)}) copy-start(f32[1024]{0:T(1024)S(1)} %convert_element_type.117) | copy-start | bytes 12292
  1001.9 363.8 %copy-start.65 = (f32[1024]{0:T(1024)}, f32[1024]{0:T(1024)S(1)}, u32[]{:S(2)}) copy-start(f32[1024]{0:T(1024)S(1)} %add_rsqrt_fusion.2) | copy-start | bytes 12292
  1005.7 170.7 %all-gather.21.cloned.1.call-start = ((), (), s32[]{:S(2)}) async-start(), calls=%async_computation.16 | async-start | bytes 6291456 | tf_op jit(solution)/shard_map/all_gather | solution.py:126
  1006.4 216.9 %all-gather.19.cloned.1.call-start = ((), (), s32[]{:S(2)}) async-start(), calls=%async_computation.14 | async-start | bytes 3063808 | tf_op jit(solution)/shard_map/all_gather | solution.py:174
  1007.2 353.3 %reduce-scatter.15.cloned.1.call-start = ((), (), s32[]{:S(2)}) async-start(), calls=%async_computation.17 | async-start | bytes 12582912 | tf_op jit(solution)/shard_map/reduce_scatter | solution.py:130
  1262.7 103.6 %copy-start.24 = (bf16[1024,1024]{1,0:T(8,128)(2,1)S(1)}, bf16[1024,1024]{1,0:T(8,128)(2,1)}, u32[]{:S(2)}) copy-start(bf16[1024,1024]{1,0:T(8,128)(2,1)} %param.29) | copy-start | bytes 6291460
  1262.8 165.3 %all-gather.23.cloned.1.call-start = ((), (), s32[]{:S(2)}) async-start(), calls=%async_computation.18 | async-start | bytes 6291456 | tf_op jit(solution)/shard_map/all_gather | solution.py:126
  1368.8 901.1 %all-reduce.33.cloned.1.call-start = ((), (), s32[]{:S(2)}) async-start(), calls=%async_computation.24 | async-start | bytes 11534336
  1399.9 872.1 %reduce-scatter.23.cloned.1.call-start = ((), (), s32[]{:S(2)}) async-start(), calls=%async_computation.22 | async-start | bytes 3063808 | tf_op jit(solution)/shard_map/reduce_scatter | solution.py:215
  1427.8 18.9 copy-start.58
  1427.8 909.2 %reduce-scatter.25.cloned.1.call-start = ((), (), s32[]{:S(2)}) async-start(), calls=%async_computation.23 | async-start | bytes 278528
  1893.8 20.4 copy-start.17
  2092.2 45.5 %copy-start.46 = (f32[1,4,32,64]{3,2,1,0:T(8,128)}, f32[1,4,32,64]{3,2,1,0:T(8,128)S(1)}, u32[]{:S(2)}) copy-start(f32[1,4,32,64]{3,2,1,0:T(8,128)S(1)} %reduce_window_sum.26) | copy-start | bytes 98308
  2092.3 45.3 %copy-start.62 = (f32[2048,4,1]{0,1,2:T(4,128)S(1)}, f32[2048,4,1]{0,1,2:T(4,128)}, u32[]{:S(2)}) copy-start(f32[2048,4,1]{0,1,2:T(4,128)} %copy-done.61) | copy-start | bytes 98308
  2092.3 45.3 %copy-start.49 = (f32[2048,4,2]{0,1,2:T(4,128)S(1)}, f32[2048,4,2]{0,1,2:T(4,128)}, u32[]{:S(2)}) copy-start(f32[2048,4,2]{0,1,2:T(4,128)} %copy-done.48) | copy-start | bytes 196612
  2092.4 45.3 %copy-start.94 = (f32[4]{0:T(128)S(1)}, f32[4]{0:T(128)}, u32[]{:S(2)}) copy-start(f32[4]{0:T(128)} %param.23) | copy-start | bytes 52
  2092.4 45.3 %copy-start.97 = (f32[4]{0:T(128)S(1)}, f32[4]{0:T(128)}, u32[]{:S(2)}) copy-start(f32[4]{0:T(128)} %copy-done.96) | copy-start | bytes 52
  2092.4 49.8 %copy-start.74 = (f32[1,4,4,128]{3,1,2,0:T(4,128)S(1)}, f32[1,4,4,128]{3,1,2,0:T(4,128)}, u32[]{:S(2)}) copy-start(f32[1,4,4,128]{3,1,2,0:T(4,128)} %copy-done.73) | copy-start | bytes 24580
  2092.4 49.8 %copy-start.76 = (f32[1,4,4,128]{3,1,2,0:T(4,128)S(1)}, f32[1,4,4,128]{3,1,2,0:T(4,128)}, u32[]{:S(2)}) copy-start(f32[1,4,4,128]{3,1,2,0:T(4,128)} %copy-done.75) | copy-start | bytes 24580
  2092.4 49.8 %copy-start.78 = (f32[1,4,4,128]{3,1,2,0:T(4,128)S(1)}, f32[1,4,4,128]{3,1,2,0:T(4,128)}, u32[]{:S(2)}) copy-start(f32[1,4,4,128]{3,1,2,0:T(4,128)} %copy-done.77) | copy-start | bytes 24580
  2092.4 49.8 %copy-start.80 = (f32[1,4,4,128]{3,1,2,0:T(4,128)S(1)}, f32[1,4,4,128]{3,1,2,0:T(4,128)}, u32[]{:S(2)}) copy-start(f32[1,4,4,128]{3,1,2,0:T(4,128)} %copy-done.79) | copy-start | bytes 24580
  2168.9 169.6 %reduce-scatter.21.cloned.1.call-start = ((), (), s32[]{:S(2)}) async-start(), calls=%async_computation.21 | async-start | bytes 2228224 | tf_op jit(solution)/shard_map/reduce_scatter | solution.py:227
  2178.8 199.0 %reduce-scatter.19.cloned.1.call-start = ((), (), s32[]{:S(2)}) async-start(), calls=%async_computation.20 | async-start | bytes 6684672 | tf_op jit(solution)/shard_map/reduce_scatter | solution.py:221
  2178.8 29.9 %copy-start.27 = (bf16[2048,1024]{1,0:T(8,128)(2,1)S(1)}, bf16[2048,1024]{1,0:T(8,128)(2,1)}, u32[]{:S(2)}) copy-start(bf16[2048,1024]{1,0:T(8,128)(2,1)} %all-gather.9.cloned.1.call-done) | copy-start | bytes 12582916
  2208.7 20.0 copy-start.29
  2228.5 249.9 %reduce-scatter.17.cloned.1.call-start = ((), (), s32[]{:S(2)}) async-start(), calls=%async_computation.19 | async-start | bytes 12582912 | tf_op jit(solution)/shard_map/reduce_scatter | solution.py:130
  2255.8 324.2 %reduce-scatter.13.cloned.1.call-start = ((), (), s32[]{:S(2)}) async-start(), calls=%async_computation.15 | async-start | bytes 12582912 | tf_op jit(solution)/shard_map/reduce_scatter | solution.py:130
  2268.4 210.1 %copy-start.13 = (bf16[1024,1024]{1,0:T(8,128)(2,1)S(1)}, bf16[1024,1024]{1,0:T(8,128)(2,1)}, u32[]{:S(2)}) copy-start(bf16[1024,1024]{1,0:T(8,128)(2,1)} %param.17) | copy-start | bytes 6291460
  2268.4 210.1 %copy-start.82 = (f32[1024]{0:T(1024)S(1)}, f32[1024]{0:T(1024)}, u32[]{:S(2)}) copy-start(f32[1024]{0:T(1024)} %copy-done.81) | copy-start | bytes 12292
  2268.4 210.1 %copy-start.84 = (f32[1024]{0:T(1024)S(1)}, f32[1024]{0:T(1024)}, u32[]{:S(2)}) copy-start(f32[1024]{0:T(1024)} %copy-done.83) | copy-start | bytes 12292
  2268.4 213.4 %copy-start.92 = (bf16[1024]{0:T(1024)(128)(2,1)S(1)}, bf16[1024]{0:T(1024)(128)(2,1)}, u32[]{:S(2)}) copy-start(bf16[1024]{0:T(1024)(128)(2,1)} %get-tuple-element.545) | copy-start | bytes 6148
  2268.4 213.4 %copy-start.103 = (bf16[256]{0:T(256)(128)(2,1)S(1)}, bf16[256]{0:T(256)(128)(2,1)}, u32[]{:S(2)}) copy-start(bf16[256]{0:T(256)(128)(2,1)} %get-tuple-element.539) | copy-start | bytes 1540
  2268.4 311.5 %copy-start.64 = (f32[1024]{0:T(1024)S(1)}, f32[1024]{0:T(1024)}, u32[]{:S(2)}) copy-start(f32[1024]{0:T(1024)} %copy-done.63) | copy-start | bytes 12292
  2268.5 311.5 %copy-start.66 = (f32[1024]{0:T(1024)S(1)}, f32[1024]{0:T(1024)}, u32[]{:S(2)}) copy-start(f32[1024]{0:T(1024)} %copy-done.65) | copy-start | bytes 12292
  2268.5 311.5 %copy-start.86 = (f32[1024]{0:T(1024)S(1)}, f32[1024]{0:T(1024)}, u32[]{:S(2)}) copy-start(f32[1024]{0:T(1024)} %copy-done.85) | copy-start | bytes 12292
  (63 other events, 421.4 us)
Sparse Core Ops, SparseCore 0:
  54.7 54.0 all-gather.8
  111.6 61.9 all-gather.10
  175.9 40.0 all-gather.12
  900.9 98.1 reduce-scatter.10
  1001.5 59.0 all-gather.16
  1062.6 55.3 all-gather.14
  1119.6 56.7 all-gather.20
  1178.9 44.3 all-gather.18
  1262.9 97.5 reduce-scatter.14
  1369.0 56.7 all-gather.22
  1429.5 131.9 all-reduce.32
  1565.1 65.0 reduce-scatter.22
  2169.0 55.3 reduce-scatter.24
  2229.1 60.6 reduce-scatter.20
  2293.5 84.1 reduce-scatter.18
  2380.0 98.4 reduce-scatter.16
  2480.6 99.3 reduce-scatter.12
where the time goes:
time: 2610 us; the launch traced here: 2600 us
  matrix products  828 us (32%)
  waiting for transfers between devices  674 us (26%)
  other arithmetic  636 us (24%)
  local copies, waits for them, and re-layouts  280 us (11%)
  blocking collectives  157 us (6%)
    reduce_scatter x4, waiting for transfers between devices, row_sums(): lax.psum_scatter(partial_value, 'tensor', scatter_dimension=0, tiled=True)  353 us
    another operation x4, other arithmetic, delta_rule(): jax.scipy.linalg.solve_triangular(system, right, lower=True, unit_diagona...  266 us
    dot_general x96, matrix products, advance(): jnp.einsum('bck,bkv->bcv', piece_w, state, precision=highest)  204 us
    dot_general x96, matrix products, advance(): jnp.einsum('bck,bcv->bkv', piece_keys, updates, precision=highest)  194 us
    all_gather x4, waiting for transfers between devices, gather_rows(): return lax.all_gather(piece, 'tensor', axis=0, tiled=True)  122 us
    dot_general x5, matrix products, contract_last(): lax.dot_general(left, right, (((1,), (1,)), ((), ())), preferred_element_...  84.9 us
    unnamed x2, blocking collectives  69.6 us
    psum x1, blocking collectives, per_device(): lax.psum((d_conv, d_decay_log, d_bias), 'dp')  62.8 us
  transfers between devices with their start and end apart: 17, of which 11 were waited for; matrix products, arithmetic and copies ran while one was open for 63% of the time, Pallas kernels for 0%

commit v1 on v0

v1 whole, which is shorter than its diff:
```python
import functools

import jax
import jax.numpy as jnp
from jax import lax
from jax.experimental import pallas as pl
from jax.experimental.pallas import tpu as pltpu
from jax.sharding import PartitionSpec as P

DK = 128
DV = 256
CONV = 4
LEN = 2048
T_PASSES = 3
K_PASSES = 3
PASSES = 1
CHUNK = 128
STEPS = 8
LANES = 128
EPSILON = 1e-06
highest = lax.Precision.HIGHEST


def rms_scale(rows):
    return rows * lax.rsqrt(jnp.mean(rows * rows, axis=-1, keepdims=True) + EPSILON)


def rms_back(rows, gain, grad):
    scale = lax.rsqrt(jnp.mean(rows * rows, axis=-1, keepdims=True) + EPSILON)
    normed = rows * scale
    weighted = grad * gain
    back = scale * (weighted - normed * jnp.mean(weighted * normed, axis=-1, keepdims=True))
    return (back, jnp.sum(grad * normed, axis=0))


def matmul(left, right):
    return jnp.dot(left, right, preferred_element_type=jnp.float32)


def contract_rows(left, right):
    return lax.dot_general(
        left, right, (((0,), (0,)), ((), ())), preferred_element_type=jnp.float32
    )


def contract_last(left, right):
    return lax.dot_general(
        left, right, (((1,), (1,)), ((), ())), preferred_element_type=jnp.float32
    )


def dot(left, right, dims, passes):
    numbers = (((dims[0],), (dims[1],)), ((), ()))

    def one(first, second):
        return lax.dot_general(first, second, numbers, preferred_element_type=jnp.float32)

    if passes == 6:
        return lax.dot_general(
            left, right, numbers, precision=highest, preferred_element_type=jnp.float32
        )
    left_high = left.astype(jnp.bfloat16)
    right_high = right.astype(jnp.bfloat16)
    total = one(left_high, right_high)
    if passes == 3:
        left_low = (left - left_high.astype(jnp.float32)).astype(jnp.bfloat16)
        right_low = (right - right_high.astype(jnp.float32)).astype(jnp.bfloat16)
        total = total + one(left_high, right_low) + one(left_low, right_high)
    return total


def indices(size):
    shape = (size, size)
    return (
        lax.broadcasted_iota(jnp.int32, shape, 0),
        lax.broadcasted_iota(jnp.int32, shape, 1),
    )


def sigmoid(value):
    return 1.0 / (1.0 + jnp.exp(-value))


def softplus(value):
    return jnp.maximum(value, 0.0) + jnp.log1p(jnp.exp(-jnp.abs(value)))


def inverses(lowers):
    size = lowers[0].shape[0]
    row, col = indices(size)
    eye = jnp.where(row == col, 1.0, 0.0)
    level = 1
    founds = [eye - jnp.where((row >> 1) == (col >> 1), lower, 0.0) for lower in lowers]
    while (1 << level) < size:
        mask = ((row >> (level + 1)) == (col >> (level + 1))) & ((row >> level) != (col >> level))
        parts = [
            dot(found, jnp.where(mask, lower, 0.0), (1, 0), T_PASSES)
            for found, lower in zip(founds, lowers)
        ]
        founds = [
            found - dot(part, found, (1, 0), T_PASSES) for found, part in zip(founds, parts)
        ]
        level += 1
    return founds


def decays(small, par):
    row, col = indices(CHUNK)
    pre = small + par[1:2]
    logdecay = par[0:1] * softplus(pre)
    cumulative = dot(jnp.where(row >= col, 1.0, 0.0), logdecay, (1, 0), 6)
    return pre, logdecay, cumulative, jnp.transpose(cumulative)


def convolve(window, conv, columns):
    total = window[5 : 5 + CHUNK, columns] * conv[0:1, columns]
    for tap in range(1, CONV):
        total = total + window[5 + tap : 5 + tap + CHUNK, columns] * conv[tap : tap + 1, columns]
    return total


def unit(rows):
    scale = lax.rsqrt(jnp.sum(rows * rows, axis=-1, keepdims=True) + EPSILON)
    return rows * scale, scale


def unit_back(normed, scale, grad):
    return scale * (grad - normed * jnp.sum(grad * normed, axis=-1, keepdims=True))


def spread_of(cumulative, flipped, head):
    row, col = indices(CHUNK)
    column = cumulative[:, 2 * head : 2 * head + 1]
    across = flipped[2 * head : 2 * head + 1, :]
    inside = row >= col
    within = jnp.where(inside, jnp.exp(jnp.where(inside, column - across, 0.0)), 0.0)
    last = column[CHUNK - 1 : CHUNK]
    return within, jnp.exp(column), jnp.exp(last - column), jnp.exp(last)


def forward_kernel(
    heads, mixed, conv, par, head_gain, gated, states, solves, state, window
):
    width = 2 * DK + DV
    per_head = width + DV
    row, col = indices(CHUNK)

    @pl.when(pl.program_id(1) == 0)
    def _():
        state[...] = jnp.zeros_like(state)
        window[CHUNK : CHUNK + STEPS] = jnp.zeros((STEPS, heads * width), jnp.float32)

    window[0:STEPS] = window[CHUNK : CHUNK + STEPS]
    states[0] = state[...]
    small_rows = mixed[:, heads * per_head :]
    pre, logdecay, cumulative, flipped = decays(small_rows, par[...])
    betas = sigmoid(small_rows)
    kept = []
    for head in range(heads):
        columns = slice(head * width, (head + 1) * width)
        window[STEPS : STEPS + CHUNK, columns] = mixed[:, head * per_head : head * per_head + width]
        mixed_rows = convolve(window, conv, columns)
        active = mixed_rows * sigmoid(mixed_rows)
        queries = unit(active[:, :DK])[0] * DK ** (-0.5)
        keys = unit(active[:, DK : 2 * DK])[0]
        beta = betas[:, 2 * head + 1 : 2 * head + 2]
        within, now, tail, whole = spread_of(cumulative, flipped, head)
        dots = dot(keys, keys, (1, 1), K_PASSES)
        lower = jnp.where(row > col, beta * dots * within, 0.0)
        kept.append((queries, keys, active[:, 2 * DK :], beta, within, now, tail, whole, lower))
    founds = inverses([entry[-1] for entry in kept])
    for head in range(heads):
        queries, keys, values, beta, within, now, tail, whole, lower = kept[head]
        solves[0, head * CHUNK : (head + 1) * CHUNK] = founds[head]
        start = state[head * DK : (head + 1) * DK]
        both = dot(jnp.concatenate([queries, keys], axis=0), start, (1, 0), PASSES)
        right = beta * (values - now * both[CHUNK:])
        updates = dot(founds[head], right, (1, 0), PASSES)
        attend = dot(queries, keys, (1, 1), PASSES) * within
        outputs = now * both[:CHUNK] + dot(attend, updates, (1, 0), PASSES)
        state[head * DK : (head + 1) * DK] = whole * start + dot(
            tail * keys, updates, (0, 0), PASSES
        )
        gate = mixed[:, head * per_head + width : (head + 1) * per_head]
        normed = outputs * lax.rsqrt(
            jnp.mean(outputs * outputs, axis=-1, keepdims=True) + EPSILON
        )
        gated[:, head * DV : (head + 1) * DV] = (
            normed * head_gain[...] * (gate * sigmoid(gate))
        ).astype(gated.dtype)


def backward_kernel(
    heads,
    mixed,
    before,
    conv,
    par,
    head_gain,
    states,
    solves,
    grads,
    d_mixed,
    d_conv,
    d_par,
    d_gain,
    d_state,
    window,
    d_window,
):
    width = 2 * DK + DV
    per_head = width + DV
    row, col = indices(CHUNK)
    lane = lax.broadcasted_iota(jnp.int32, (CHUNK, LANES), 1)
    step = pl.program_id(1)

    @pl.when((pl.program_id(0) == 0) & (step == 0))
    def _():
        d_conv[...] = jnp.zeros_like(d_conv)
        d_par[...] = jnp.zeros_like(d_par)
        d_gain[...] = jnp.zeros_like(d_gain)

    @pl.when(step == 0)
    def _():
        d_state[...] = jnp.zeros_like(d_state)
        d_window[0:STEPS] = jnp.zeros((STEPS, heads * width), jnp.float32)

    d_window[CHUNK : CHUNK + STEPS] = d_window[0:STEPS]
    first = step == pl.num_programs(1) - 1
    small_rows = mixed[:, heads * per_head :]
    pre, logdecay, cumulative, flipped = decays(small_rows, par[...])
    betas = sigmoid(small_rows)
    d_cumulative = jnp.zeros_like(small_rows)
    d_betas = jnp.zeros_like(small_rows)
    d_last = jnp.zeros((1, LANES), jnp.float32)
    for head in range(heads):
        columns = slice(head * width, (head + 1) * width)
        lead = slice(head * per_head, head * per_head + width)
        window[0:STEPS, columns] = jnp.where(first, 0.0, before[:, lead])
        window[STEPS : STEPS + CHUNK, columns] = mixed[:, lead]
        mixed_rows = convolve(window, conv, columns)
        sigma = sigmoid(mixed_rows)
        active = mixed_rows * sigma
        query_units, query_scale = unit(active[:, :DK])
        queries = query_units * DK ** (-0.5)
        keys, key_scale = unit(active[:, DK : 2 * DK])
        values = active[:, 2 * DK :]
        beta = betas[:, 2 * head + 1 : 2 * head + 2]
        within, now, tail, whole = spread_of(cumulative, flipped, head)
        dots = dot(keys, keys, (1, 1), K_PASSES)
        found = solves[0, head * CHUNK : (head + 1) * CHUNK]
        start = states[0, head * DK : (head + 1) * DK]
        pair = jnp.concatenate([queries, keys], axis=0)
        both = dot(pair, start, (1, 0), PASSES)
        query_start = both[:CHUNK]
        key_start = now * both[CHUNK:]
        free = values - key_start
        updates = dot(found, beta * free, (1, 0), PASSES)
        query_dots = dot(queries, keys, (1, 1), PASSES)
        attend = query_dots * within
        outputs = now * query_start + dot(attend, updates, (1, 0), PASSES)

        gate = mixed[:, head * per_head + width : (head + 1) * per_head]
        gate_sigma = sigmoid(gate)
        silu = gate * gate_sigma
        scale = lax.rsqrt(jnp.mean(outputs * outputs, axis=-1, keepdims=True) + EPSILON)
        normed = outputs * scale
        grad = grads[:, head * DV : (head + 1) * DV]
        gain = head_gain[...]
        along = grad * normed
        d_mixed[:, head * per_head + width : (head + 1) * per_head] = (
            along * gain * (gate_sigma * (1.0 + gate * (1.0 - gate_sigma)))
        ).astype(d_mixed.dtype)
        d_gain[0:1] += jnp.sum(along * silu, axis=0, keepdims=True)
        weighted = grad * gain * silu
        d_out = scale * (
            weighted - normed * jnp.mean(weighted * normed, axis=-1, keepdims=True)
        )

        d_next = d_state[head * DK : (head + 1) * DK]
        tail_keys = tail * keys
        d_updates = dot(attend, d_out, (0, 0), PASSES) + dot(tail_keys, d_next, (1, 0), PASSES)
        d_right = dot(found, d_updates, (0, 0), PASSES)
        d_values = beta * d_right
        d_pair = jnp.concatenate([now * d_out, -now * d_values], axis=0)
        d_state[head * DK : (head + 1) * DK] = whole * d_next + dot(
            pair, d_pair, (0, 0), PASSES
        )
        d_attend = dot(d_out, updates, (1, 1), PASSES) * within
        d_lower = -jnp.where(row > col, dot(d_right, updates, (1, 1), PASSES), 0.0) * within
        d_dots = beta * d_lower
        d_units = dot(d_pair, start, (1, 1), PASSES)
        d_tail_keys = dot(updates, d_next, (1, 1), PASSES)
        d_queries = d_units[:CHUNK] + dot(d_attend, keys, (1, 0), PASSES)
        d_keys = (
            d_units[CHUNK:]
            + dot(d_attend, queries, (0, 0), PASSES)
            + dot(d_dots + jnp.transpose(d_dots), keys, (1, 0), PASSES)
            + tail * d_tail_keys
        )
        d_beta = jnp.sum(d_right * free, axis=-1, keepdims=True) + jnp.sum(
            d_lower * dots, axis=-1, keepdims=True
        )
        moved = d_dots * dots + d_attend * query_dots
        tail_part = jnp.sum(d_tail_keys * tail_keys, axis=-1, keepdims=True)
        d_cum = (
            jnp.sum(moved - jnp.transpose(moved), axis=-1, keepdims=True)
            + now * jnp.sum(d_out * query_start, axis=-1, keepdims=True)
            - jnp.sum(d_values * key_start, axis=-1, keepdims=True)
            - tail_part
        )
        ending = jnp.sum(tail_part, axis=0, keepdims=True) + whole * jnp.sum(
            jnp.sum(d_next * start, axis=-1, keepdims=True), axis=0, keepdims=True
        )
        d_cumulative = jnp.where(lane == 2 * head, d_cum, d_cumulative)
        d_last = jnp.where(lane[0:1] == 2 * head, ending, d_last)
        d_betas = jnp.where(lane == 2 * head + 1, d_beta, d_betas)

        d_active = jnp.concatenate(
            [
                unit_back(query_units, query_scale, d_queries * DK ** (-0.5)),
                unit_back(keys, key_scale, d_keys),
                d_values,
            ],
            axis=1,
        )
        d_rows = d_active * (sigma * (1.0 + mixed_rows * (1.0 - sigma)))
        d_window[0:CHUNK, columns] = d_rows
        d_lead = d_window[3 : 3 + CHUNK, columns] * conv[0:1, columns]
        for tap in range(CONV):
            if tap:
                d_lead = d_lead + (
                    d_window[3 - tap : 3 - tap + CHUNK, columns] * conv[tap : tap + 1, columns]
                )
            d_conv[tap : tap + 1, columns] += jnp.sum(
                d_rows * window[5 + tap : 5 + tap + CHUNK, columns], axis=0, keepdims=True
            )
        d_mixed[:, lead] = d_lead.astype(d_mixed.dtype)

    d_logdecay = dot(jnp.where(row <= col, 1.0, 0.0), d_cumulative, (1, 0), 6) + d_last
    d_logit = d_logdecay * par[0:1] * sigmoid(pre)
    d_mixed[:, heads * per_head :] = (d_logit + d_betas * betas * (1.0 - betas)).astype(
        d_mixed.dtype
    )
    d_par[0:1] += jnp.sum(d_logdecay * logdecay, axis=0, keepdims=True)
    d_par[1:2] += jnp.sum(d_logit, axis=0, keepdims=True)


def core_specs(heads, chunks, backward):
    def at(seq, step):
        place = chunks - 1 - step if backward else step
        return seq * chunks + place

    def rows(columns):
        return pl.BlockSpec((CHUNK, columns), lambda seq, step: (at(seq, step), 0))

    def slab(height, columns):
        return pl.BlockSpec((1, height, columns), lambda seq, step: (at(seq, step), 0, 0))

    def fixed(height, columns):
        return pl.BlockSpec((height, columns), lambda seq, step: (0, 0))

    return at, rows, slab, fixed


def core_forward(mixed, conv, par, head_gain, heads):
    count = mixed.shape[0]
    seqs, chunks = count // LEN, LEN // CHUNK
    width = 2 * DK + DV
    at, rows, slab, fixed = core_specs(heads, chunks, False)
    return pl.pallas_call(
        functools.partial(forward_kernel, heads),
        grid=(seqs, chunks),
        in_specs=[
            rows(mixed.shape[1]),
            fixed(*conv.shape),
            fixed(*par.shape),
            fixed(*head_gain.shape),
        ],
        out_specs=[rows(heads * DV), slab(heads * DK, DV), slab(heads * CHUNK, CHUNK)],
        out_shape=[
            jax.ShapeDtypeStruct((count, heads * DV), jnp.bfloat16),
            jax.ShapeDtypeStruct((seqs * chunks, heads * DK, DV), jnp.float32),
            jax.ShapeDtypeStruct((seqs * chunks, heads * CHUNK, CHUNK), jnp.float32),
        ],
        scratch_shapes=[
            pltpu.VMEM((heads * DK, DV), jnp.float32),
            pltpu.VMEM((CHUNK + STEPS, heads * width), jnp.float32),
        ],
        compiler_params=pltpu.CompilerParams(vmem_limit_bytes=40 * 2**20),
        cost_estimate=pl.CostEstimate(
            flops=count * heads * 600000, bytes_accessed=count * heads * 10000, transcendentals=0
        ),
        name="core_forward",
    )(mixed, conv, par, head_gain)


def core_backward(mixed, conv, par, head_gain, states, solves, grads, heads):
    count = mixed.shape[0]
    seqs, chunks = count // LEN, LEN // CHUNK
    width = 2 * DK + DV
    at, rows, slab, fixed = core_specs(heads, chunks, True)

    def earlier(seq, step):
        return (jnp.maximum(at(seq, step) * (CHUNK // STEPS) - 1, 0), 0)

    return pl.pallas_call(
        functools.partial(backward_kernel, heads),
        grid=(seqs, chunks),
        in_specs=[
            rows(mixed.shape[1]),
            pl.BlockSpec((STEPS, mixed.shape[1]), earlier),
            fixed(*conv.shape),
            fixed(*par.shape),
            fixed(*head_gain.shape),
            slab(heads * DK, DV),
            slab(heads * CHUNK, CHUNK),
            rows(heads * DV),
        ],
        out_specs=[
            rows(mixed.shape[1]),
            fixed(STEPS, conv.shape[1]),
            fixed(*par.shape),
            fixed(STEPS, DV),
        ],
        out_shape=[
            jax.ShapeDtypeStruct(mixed.shape, jnp.bfloat16),
            jax.ShapeDtypeStruct((STEPS, conv.shape[1]), jnp.float32),
            jax.ShapeDtypeStruct(par.shape, jnp.float32),
            jax.ShapeDtypeStruct((STEPS, DV), jnp.float32),
        ],
        scratch_shapes=[
            pltpu.VMEM((heads * DK, DV), jnp.float32),
            pltpu.VMEM((CHUNK + STEPS, heads * width), jnp.float32),
            pltpu.VMEM((CHUNK + STEPS, heads * width), jnp.float32),
        ],
        compiler_params=pltpu.CompilerParams(vmem_limit_bytes=48 * 2**20),
        cost_estimate=pl.CostEstimate(
            flops=count * heads * 900000, bytes_accessed=count * heads * 12000, transcendentals=0
        ),
        name="core_backward",
    )(mixed, mixed, conv, par, head_gain, states, solves, grads)


def spread_lanes(pairs, lanes):
    heads = pairs.shape[0]
    placed = jnp.stack([pairs, jnp.zeros_like(pairs)], axis=1).reshape(1, 2 * heads)
    return jnp.pad(placed, ((0, 0), (0, lanes - 2 * heads)))


def gather_rows(piece):
    return lax.all_gather(piece, "tensor", axis=0, tiled=True)


def row_sums(rows, product):
    size = lax.axis_size("tensor")
    place = lax.axis_index("tensor")
    piece = rows.shape[0] // size

    def part(owner):
        return product(lax.dynamic_slice_in_dim(rows, owner * piece, piece, axis=0))

    arrived = []
    for shift in range(1, size):
        sent = part((place + shift) % size).astype(jnp.bfloat16)
        pairs = [(source, (source + shift) % size) for source in range(size)]
        arrived.append(lax.ppermute(sent, "tensor", pairs))
    total = part(place)
    for received in arrived:
        total = total + received.astype(jnp.float32)
    return total


def scatter_sum(partial_value, axis):
    return lax.psum_scatter(
        partial_value.astype(jnp.bfloat16), "dp", scatter_dimension=axis, tiled=True
    ).astype(jnp.float32)


def per_device(
    inputs,
    attn_gain,
    w_mix_in,
    w_decay_beta,
    conv_weight,
    a_log,
    dt_bias,
    head_gain,
    w_out,
    mlp_gain,
    w_gate_up,
    w_down,
    cotangent,
):
    slices, heads = w_mix_in.shape[:2]
    units = w_gate_up.shape[2]
    width = inputs.shape[1]
    columns = heads * (2 * DK + 2 * DV)
    value_width = head_gain.shape[0]
    padded_gain = jnp.pad(head_gain, (0, slices - value_width))
    packed = jnp.concatenate(
        [
            w_mix_in.reshape(slices, columns),
            w_decay_beta.reshape(slices, 2 * heads),
            jnp.stack([attn_gain, mlp_gain, padded_gain], axis=1),
            jnp.zeros((slices, LANES - 2 * heads - 3), jnp.bfloat16),
        ],
        axis=1,
    )
    all_inputs = gather_rows(inputs)
    mix_matrix = lax.all_gather(packed, "dp", axis=0, tiled=True)
    gains = mix_matrix[:, columns + 2 * heads : columns + 2 * heads + 3].astype(jnp.float32)
    attn_scale = gains[:, 0]
    mlp_scale = gains[:, 1]
    head_scale = gains[:, 2].reshape(-1, slices)[:, :value_width].reshape(1, -1)
    out_matrix = lax.all_gather(w_out.reshape(heads * DV, -1), "dp", axis=1, tiled=True)
    gate_up_matrix = lax.all_gather(
        w_gate_up.reshape(slices, 2 * units), "dp", axis=0, tiled=True
    )
    down_full = lax.all_gather(w_down, "dp", axis=1, tiled=True)
    back_rows = gather_rows(cotangent)

    residual = inputs.astype(jnp.float32)
    normed_one = (rms_scale(all_inputs.astype(jnp.float32)) * attn_scale).astype(jnp.bfloat16)
    mixed = matmul(normed_one, mix_matrix)
    conv = conv_weight.reshape(CONV, -1)
    par = jnp.concatenate(
        [
            spread_lanes(-jnp.exp(a_log), LANES),
            spread_lanes(dt_bias, LANES),
            jnp.zeros((STEPS - 2, LANES), jnp.float32),
        ],
        axis=0,
    )
    gated, states, solves = core_forward(mixed, conv, par, head_scale, heads)
    middle = residual + row_sums(gated, lambda rows: matmul(rows, out_matrix))
    piece_two = (rms_scale(middle) * mlp_scale).astype(jnp.bfloat16)
    normed_two = gather_rows(piece_two)
    both = matmul(normed_two, gate_up_matrix)
    gate = both[:, :units]
    up = both[:, units:]
    hidden = (jax.nn.silu(gate) * up).astype(jnp.bfloat16)
    d_hidden = contract_last(back_rows, down_full)
    sigmoid_gate = jax.nn.sigmoid(gate)
    d_gate = d_hidden * up * sigmoid_gate * (1.0 + gate * (1.0 - sigmoid_gate))
    d_up = d_hidden * gate * sigmoid_gate
    d_both = jnp.concatenate([d_gate, d_up], axis=1).astype(jnp.bfloat16)
    d_normed_two = row_sums(d_both, lambda rows: contract_last(rows, gate_up_matrix))
    gate_up_sum = scatter_sum(contract_rows(normed_two, d_both), 0)
    down_sum = scatter_sum(contract_rows(hidden, back_rows), 1)
    d_middle, grad_mlp_gain = rms_back(middle, mlp_scale, d_normed_two)
    d_middle = d_middle + cotangent.astype(jnp.float32)
    middle_rows = gather_rows(d_middle.astype(jnp.bfloat16))
    hidden_late, middle_rows = lax.optimization_barrier((hidden, middle_rows))
    block_output = (middle + row_sums(hidden_late, lambda rows: matmul(rows, down_full))).astype(
        jnp.bfloat16
    )
    out_sum = scatter_sum(contract_rows(gated, middle_rows), 1)
    d_gated = contract_last(middle_rows, out_matrix)
    d_mixed, d_conv, d_par, d_head = core_backward(
        mixed, conv, par, head_scale, states, solves, d_gated, heads
    )
    mix_sum = scatter_sum(contract_rows(normed_one, d_mixed), 0)
    d_normed_one = row_sums(d_mixed, lambda rows: contract_last(rows, mix_matrix))
    d_inputs, grad_attn_gain = rms_back(residual, attn_scale, d_normed_one)
    input_grad = (d_inputs + d_middle).astype(jnp.bfloat16)

    own = jnp.concatenate([d_conv[:CONV].reshape(-1), d_par[:2].reshape(-1)])
    size = lax.axis_size("tensor")
    place = lax.axis_index("tensor")
    spread = jnp.where(jnp.arange(size)[:, None] == place, own[None], 0.0).reshape(-1)
    sums = lax.psum(
        jnp.concatenate([grad_attn_gain, grad_mlp_gain, d_head[0], spread]), ("dp", "tensor")
    )
    mine = lax.dynamic_slice_in_dim(sums[2 * width + DV :], place * own.shape[0], own.shape[0])
    conv_size = d_conv.shape[1] * CONV
    decays_sum = mine[conv_size:].reshape(2, LANES)[:, : 2 * heads : 2]
    index = lax.axis_index("dp")

    def share(values, length):
        return lax.dynamic_slice_in_dim(values, index * length, length)

    return (
        block_output,
        input_grad,
        share(sums[:width], slices),
        mix_sum[:, :columns].reshape(slices, heads, -1),
        mix_sum[:, columns : columns + 2 * heads].reshape(slices, heads, 2),
        mine[:conv_size].reshape(conv_weight.shape),
        decays_sum[0],
        decays_sum[1],
        share(sums[2 * width : 2 * width + DV], value_width),
        out_sum.reshape(heads, DV, -1),
        share(sums[width : 2 * width], slices),
        gate_up_sum.reshape(slices, 2, units),
        down_sum,
    )


def solution(mesh):
    in_specs = (
        P(("dp", "tensor"), None),
        P("dp"),
        P("dp", "tensor", None),
        P("dp", "tensor", None),
        P(None, "tensor", None),
        P("tensor"),
        P("tensor"),
        P("dp"),
        P("tensor", None, "dp"),
        P("dp"),
        P("dp", None, "tensor"),
        P("tensor", "dp"),
        P(("dp", "tensor"), None),
    )
    out_specs = (
        P(("dp", "tensor"), None),
        P(("dp", "tensor"), None),
        P("dp"),
        P("dp", "tensor", None),
        P("dp", "tensor", None),
        P(None, "tensor", None),
        P("tensor"),
        P("tensor"),
        P("dp"),
        P("tensor", None, "dp"),
        P("dp"),
        P("dp", None, "tensor"),
        P("tensor", "dp"),
    )
    return jax.shard_map(
        per_device, mesh=mesh, in_specs=in_specs, out_specs=out_specs, check_vma=False
    )
```

time: 2610 us -> 1220 us (0.47)
  other arithmetic: 636 us -> 21.8 us
  matrix products: 828 us -> 219 us
  local copies, waits for them, and re-layouts: 280 us -> 39.5 us
  Pallas kernels: 0 us -> 214 us
  blocking collectives: 157 us -> 0 us
  waiting for transfers between devices: 674 us -> 706 us
    dot_general x205 -> x0, matrix products: 584 us -> none  [the longest x96 204 us: advance(): jnp.einsum('bck,bkv->bcv', piece_w, state, precision=highest)]
    another operation x7 -> x1, other arithmetic: 268 us -> 0.01 us  [spread_lanes(): jnp.stack([pairs, jnp.zeros_like(pairs)], axis=1).reshape(1, 2 * heads)]
    pallas_call x0 -> x2, Pallas kernels: none -> 214 us  [the longest x1 135 us: core_backward(): pl.pallas_call(functools.partial(backward_kernel, heads), grid=(seqs, chu...]
    ppermute x0 -> x4, waiting for transfers between devices: none -> 168 us  [row_sums(): arrived.append(lax.ppermute(sent, 'tensor', pairs))]
    reduce_scatter x7 -> x4, waiting for transfers between devices: 390 us -> 233 us  [scatter_sum(): lax.psum_scatter(partial_value.astype(jnp.bfloat16), 'dp', scatter_dimens...]
    reduce_sum x43 -> x1, other arithmetic: 116 us -> 0.48 us  [rms_back(): scale = lax.rsqrt(jnp.mean(rows * rows, axis=-1, keepdims=True) + EPSILON)]
    mul x12 -> x0, other arithmetic: 101 us -> none  [the longest x1 38.7 us: mix_core(): active = jax.nn.silu(mixed).reshape(count, heads, conv_width)]
    unnamed x2 -> x0, blocking collectives: 69.6 us -> none
  transfers between devices with their start and end apart: 17 -> 17, of which waited for: 11 -> 14; matrix products, arithmetic and copies ran while one was open for 63% -> 17% of each run, Pallas kernels for 0% -> 18%
where the time goes in v1:
time: 1220 us
  waiting for transfers between devices  706 us (58%)
  matrix products  219 us (18%)
  Pallas kernels  214 us (18%)
  local copies, waits for them, and re-layouts  39.5 us (3%)
  other arithmetic  21.8 us (2%)
  between operations  14.5 us (1%)
    reduce_scatter x4, waiting for transfers between devices, scatter_sum(): lax.psum_scatter(partial_value.astype(jnp.bfloat16), 'dp', scatter_dimens...  233 us
    all_gather x4, waiting for transfers between devices, gather_rows(): return lax.all_gather(piece, 'tensor', axis=0, tiled=True)  189 us
    ppermute x4, waiting for transfers between devices, row_sums(): arrived.append(lax.ppermute(sent, 'tensor', pairs))  168 us
    pallas_call x1, Pallas kernels, core_backward(): pl.pallas_call(functools.partial(backward_kernel, heads), grid=(seqs, chu...  135 us
    dot_general x6, matrix products, contract_last(): lax.dot_general(left, right, (((1,), (1,)), ((), ())), preferred_element_...  88.5 us
    pallas_call x1, Pallas kernels, core_forward(): pl.pallas_call(functools.partial(forward_kernel, heads), grid=(seqs, chun...  79.1 us
    dot_general x6, matrix products, matmul(): return jnp.dot(left, right, preferred_element_type=jnp.float32)  68.7 us
    all_gather x1, waiting for transfers between devices, per_device(): mix_matrix = lax.all_gather(packed, 'dp', axis=0, tiled=True)  63.2 us
  transfers between devices with their start and end apart: 17, of which 14 were waited for; matrix products, arithmetic and copies ran while one was open for 17% of the time, Pallas kernels for 18%

profile of v1, /device:TPU:0, one launch (start us, length us, event | category | flops | bytes accessed | tf_op | source)
XLA Modules:
  0.0 1218.8 jit_solution(410550148511137305)
XLA Ops:
  7.3 0.7 all-gather.9.cloned.1.call-update
  8.0 1.0 copy.122
  9.8 0.8 copy.89
  10.6 0.8 copy.90
  11.4 0.8 copy.91
  12.1 0.9 concatenate.16
  13.8 0.8 copy.124
  15.3 53.8 %all-gather.9.cloned.1.call-done = bf16[2048,1024]{1,0:T(8,128)(2,1)} async-done(((bf16[1024,1024]{1,0:T(8,128)(2,1)}), bf16[2048,1024]{1,0:T(8,128)(2,1)}) %all-gather.9.cloned.1.call-update) | async-done | bytes 4194320 | tf_op jit(solution)/shard_map/all_gather | solution.py:452
  69.1 3.1 fusion.1
  72.2 63.2 %all-gather.11.cloned.1.call-done = bf16[1024,3200]{1,0:T(8,128)(2,1)} async-done(((bf16[64,3200]{1,0:T(8,128)(2,1)}), bf16[1024,3200]{1,0:T(8,128)(2,1)}) %all-gather.11.cloned.1.call-update) | async-done | bytes 6553616 | tf_op jit(solution)/shard_map/all_gather | solution.py:511
  135.4 1.1 slice_convert_fusion
  136.5 0.8 slice_reduce_fusion
  137.4 22.0 %fusion.50.mixed.before = f32[2048,3200]{1,0:T(8,128)} fusion(bf16[1024,3200]{1,0:T(8,128)(2,1)} %all-gather.11.cloned.1.call-done, bf16[2048,1024]{1,0:T(8,128)(2,1)} %all-gather.9.cloned.1.call-done, f32[1024]{0:T(1024)S(1)} %get-tuple-element.89, f32[2048]{0:T(1024)S(1)} %add_rsqrt_fusion), kind=kOutput, calls=%fused_computation.60 | convolution fusion | flops 13430161408 | bytes 36974592 | tf_op jit(solution)/shard_map/dot_general | solution.py:37
  159.4 79.1 %core_forward.1 = (bf16[2048,1024]{1,0:T(8,128)(2,1)S(1)}, f32[16,512,256]{2,1,0:T(8,128)}, f32[16,512,128]{2,1,0:T(8,128)S(1)}) custom-call(f32[2048,3200]{1,0:T(8,128)} %fusion.50.mixed.before, f32[4,2048]{1,0:T(4,128)S(1)} %bitcast.55, f32[8,128]{1,0:T(8,128)S(1)} %fusion.52.par, f32[1,256]{1,0:T(1,128)S(1)} %reshape.136.head_gain), custom_call_target="tpu_custom_call" | custom-call | flops 4915200000 | bytes 81920000 | tf_op jit(solution)/shard_map/core_forward/pallas_call | solution.py:371
  238.5 2.0 copy-done
  240.5 2.0 copy-done.2
  242.5 5.9 fusion.33
  248.4 1.5 collective-permute-start
  249.9 3.1 copy.88
  253.0 43.5 %collective-permute-done = bf16[1024,1024]{0,1:T(8,128)(2,1)} collective-permute-done((bf16[1024,1024]{0,1:T(8,128)(2,1)}, bf16[1024,1024]{0,1:T(8,128)(2,1)}, u32[]{:S(2)}, u32[]{:S(2)}) %collective-permute-start) | collective-permute-done | bytes 2097184 | tf_op jit(solution)/shard_map/ppermute | solution.py:467
  296.5 5.5 multiply_reduce_fusion.2
  302.0 1.9 copy-done.3
  304.0 1.7 multiply_convert_fusion.3
  306.4 0.7 all-gather.21.cloned.1.call-update
  307.1 54.1 %all-gather.15.cloned.1.call-done = bf16[2048,1024]{0,1:T(8,128)(2,1)} async-done(((bf16[1024,1024]{0,1:T(8,128)(2,1)}), bf16[2048,1024]{0,1:T(8,128)(2,1)}) %all-gather.15.cloned.1.call-update) | async-done | bytes 4194320 | tf_op jit(solution)/shard_map/all_gather | solution.py:452
  361.2 19.9 %fusion.67 = f32[2048,2816]{1,0:T(8,128)} fusion(bf16[2048,1024]{0,1:T(8,128)(2,1)} %all-gather.15.cloned.1.call-done, bf16[1024,2816]{1,0:T(8,128)(2,1)} %all-gather.17.cloned.1.call-done), kind=kOutput, calls=%fused_computation.101 | convolution fusion | flops 11811160064 | bytes 33030144 | tf_op jit(solution)/shard_map/dot_general | solution.py:37
  381.1 38.2 %all-gather.19.cloned.1.call-done = bf16[2048,1024]{1,0:T(8,128)(2,1)} async-done(((bf16[1024,1024]{1,0:T(8,128)(2,1)}), bf16[2048,1024]{1,0:T(8,128)(2,1)}) %all-gather.19.cloned.1.call-update) | async-done | bytes 4194320 | tf_op jit(solution)/shard_map/all_gather | solution.py:452
  419.4 46.7 %all-gather.21.cloned.1.call-done = bf16[1408,1024]{0,1:T(8,128)(2,1)} async-done(((bf16[1408,64]{0,1:T(8,128)(2,1)}), bf16[1408,1024]{0,1:T(8,128)(2,1)}) %all-gather.21.cloned.1.call-update) | async-done | bytes 2883600 | tf_op jit(solution)/shard_map/all_gather | solution.py:520
  466.1 21.5 %multiply_convert_fusion = (bf16[2048,1408]{1,0:T(8,128)(2,1)}, bf16[2048,1408]{1,0:T(8,128)(2,1)}, bf16[2048,1408]{1,0:T(8,128)(2,1)}) fusion(f32[2048,2816]{1,0:T(8,128)} %fusion.67, bf16[2048,1024]{1,0:T(8,128)(2,1)} %all-gather.19.cloned.1.call-done, bf16[1408,1024]{0,1:T(8,128)(2,1)} %all-gather.21.cloned.1.call-done), kind=kOutput, calls=%fused_computation.6 | convolution fusion | flops 5951717376 | bytes 47448064 | tf_op jit(solution)/shard_map/dot_general | solution.py:47
  487.5 20.5 %fusion.36 = bf16[1024,1024]{0,1:T(8,128)(2,1)} fusion(bf16[1024,2816]{1,0:T(8,128)(2,1)} %all-gather.17.cloned.1.call-done, s32[]{:T(128)S(6)} %select_n.45, bf16[2048,1408]{1,0:T(8,128)(2,1)} %get-tuple-element.93, bf16[2048,1408]{1,0:T(8,128)(2,1)} %get-tuple-element.92), kind=kOutput, calls=%fused_computation.56 | convolution fusion | flops 5918162944 | bytes 19398660 | tf_op jit(solution)/shard_map/dot_general | solution.py:47
  508.1 1.5 collective-permute-start.1
  509.5 3.9 copy.101
  513.5 42.7 %collective-permute-done.1 = bf16[1024,1024]{0,1:T(8,128)(2,1)} collective-permute-done((bf16[1024,1024]{0,1:T(8,128)(2,1)}, bf16[1024,1024]{0,1:T(8,128)(2,1)}, u32[]{:S(2)}, u32[]{:S(2)}) %collective-permute-start.1) | collective-permute-done | bytes 2097184 | tf_op jit(solution)/shard_map/ppermute | solution.py:467
  556.2 11.5 multiply_reduce_fusion
  567.7 5.2 fusion.65
  573.6 11.3 convolution_convert_fusion.1
  585.0 43.3 %all-gather.23.cloned.1.call-done = bf16[2048,1024]{0,1:T(8,128)(2,1)} async-done(((bf16[1024,1024]{0,1:T(8,128)(2,1)}), bf16[2048,1024]{0,1:T(8,128)(2,1)}) %all-gather.23.cloned.1.call-update) | async-done | bytes 4194320 | tf_op jit(solution)/shard_map/all_gather | solution.py:452
  628.2 10.9 fusion.68.grads
  639.2 134.7 %core_backward.1 = (bf16[2048,3200]{1,0:T(8,128)(2,1)}, f32[8,2048]{1,0:T(8,128)S(1)}, f32[8,128]{1,0:T(8,128)S(1)}, f32[8,256]{1,0:T(8,128)S(1)}) custom-call(f32[2048,3200]{1,0:T(8,128)} %fusion.50.mixed.before, f32[2048,3200]{1,0:T(8,128)} %fusion.50.mixed.before, f32[4,2048]{1,0:T(4,128)S(1)} %bitcast.56, f32[8,128]{1,0:T(8,128)S(1)} %fusion.52.par, ...), custom_call_target="tpu_custom_call" | custom-call | flops 7372800000 | bytes 98304000 | tf_op jit(solution)/shard_map/core_backward/pallas_call | solution.py:407
  773.9 10.3 fusion.39
  784.7 47.2 %collective-permute-done.3 = bf16[1024,1024]{0,1:T(8,128)(2,1)} collective-permute-done((bf16[1024,1024]{0,1:T(8,128)(2,1)}, bf16[1024,1024]{0,1:T(8,128)(2,1)}, u32[]{:S(2)}, u32[]{:S(2)}) %collective-permute-start.3) | collective-permute-done | bytes 2097184 | tf_op jit(solution)/shard_map/ppermute | solution.py:467
  831.9 13.7 %fusion.23 = (f32[1024]{0:T(1024)S(1)}, f32[1024]{0:T(1024)S(1)}, f32[1024,1024]{0,1:T(8,128)}) fusion(bf16[1024,1024]{0,1:T(8,128)(2,1)S(1)} %copy.88, f32[1024]{0:T(1024)S(1)} %add_rsqrt_fusion.1, bf16[1024,1024]{0,1:T(8,128)(2,1)} %collective-permute-done.3, f32[1024]{0:T(1024)S(1)} %copy-done.10, bf16[1024,3200]{1,0:T(8,128)(2,1)} %all-gather.11.cloned.1.call-done, ...), kind=kOutput, calls=%fused_computation.36 | convolution fusion | flops 6720321536 | bytes 21512196 | tf_op jit(solution)/shard_map/dot_general | solution.py:47
  846.4 19.2 %fusion.17 = bf16[1024,2816]{1,0:T(8,128)(2,1)} fusion(bf16[2048,1024]{0,1:T(8,128)(2,1)} %all-gather.15.cloned.1.call-done, bf16[2048,1408]{1,0:T(8,128)(2,1)} %get-tuple-element.92, bf16[2048,1408]{1,0:T(8,128)(2,1)} %get-tuple-element.93), kind=kOutput, calls=%fused_computation.30 | convolution fusion | flops 11837112320 | bytes 21495808 | tf_op jit(solution)/shard_map/dot_general | solution.py:41
  865.6 9.3 convolution_convert_fusion.2
  875.0 21.9 %convolution_convert_fusion = bf16[1024,3200]{1,0:T(8,128)(2,1)} fusion(bf16[2048,3200]{1,0:T(8,128)(2,1)} %get-tuple-element.27, bf16[2048,1024]{1,0:T(8,128)(2,1)} %all-gather.9.cloned.1.call-done, f32[1024]{0:T(1024)S(1)} %copy-done.10, f32[2048]{0:T(1024)S(1)} %copy-done.12), kind=kOutput, calls=%fused_computation.15 | convolution fusion | flops 13433438208 | bytes 23867392 | tf_op jit(solution)/shard_map/dot_general | solution.py:41
  896.9 7.5 fusion.42
  904.8 1.7 convert_element_type.103
  906.4 6.7 fusion.22
  913.2 3.9 copy.108
  917.1 34.3 %collective-permute-done.2 = bf16[1024,1024]{0,1:T(8,128)(2,1)} collective-permute-done((bf16[1024,1024]{0,1:T(8,128)(2,1)}, bf16[1024,1024]{0,1:T(8,128)(2,1)}, u32[]{:S(2)}, u32[]{:S(2)}) %collective-permute-start.2) | collective-permute-done | bytes 2097184 | tf_op jit(solution)/shard_map/ppermute | solution.py:467
  951.4 7.9 add_convert_fusion
  959.3 2.6 copy.107
  961.9 3.7 all-reduce.7.cloned.1.call-done
  965.6 0.9 slice.105
  967.4 0.7 fusion.66
  971.0 82.6 %reduce-scatter.9.cloned.1.call-done = bf16[64,2816]{1,0:T(8,128)(2,1)} async-done(((bf16[1024,2816]{1,0:T(8,128)(2,1)}), bf16[64,2816]{1,0:T(8,128)(2,1)}) %reduce-scatter.9.cloned.1.call-update) | async-done | bytes 360464 | tf_op jit(solution)/shard_map/reduce_scatter | solution.py:475
  1053.6 2.2 reshape.151
  1055.8 62.5 %reduce-scatter.7.cloned.1.call-done = bf16[1024,64]{0,1:T(8,128)(2,1)} async-done(((bf16[1024,1024]{0,1:T(8,128)(2,1)}), bf16[1024,64]{0,1:T(8,128)(2,1)}) %reduce-scatter.7.cloned.1.call-update) | async-done | bytes 131088 | tf_op jit(solution)/shard_map/reduce_scatter | solution.py:475
  1118.4 0.9 reshape.148
  1119.3 0.7 copy.127
  1120.0 88.3 %reduce-scatter.5.cloned.1.call-done = bf16[64,3200]{1,0:T(8,128)(2,1)} async-done(((bf16[1024,3200]{1,0:T(8,128)(2,1)}), bf16[64,3200]{1,0:T(8,128)(2,1)}) %reduce-scatter.5.cloned.1.call-update) | async-done | bytes 409616 | tf_op jit(solution)/shard_map/reduce_scatter | solution.py:475
  1208.3 1.0 slice.103
  1209.4 1.3 reshape.141
  1210.7 0.7 slice.104
  (103 shorter events, 10.0 us)
Async XLA Ops:
  7.2 5.9 copy-start.7
  7.2 6.6 copy-start.6
  7.2 7.5 copy-start.8
  7.2 7.5 copy-start.14
  7.2 7.7 copy-start.13
  7.2 61.9 %all-gather.9.cloned.1.call-start = ((), (), s32[]{:S(2)}) async-start(), calls=%async_computation.4 | async-start | bytes 6291456 | tf_op jit(solution)/shard_map/all_gather | solution.py:452
  8.0 127.4 %all-gather.11.cloned.1.call-start = ((), (), s32[]{:S(2)}) async-start(), calls=%async_computation.5 | async-start | bytes 6963200 | tf_op jit(solution)/shard_map/all_gather | solution.py:511
  13.0 229.5 %all-gather.13.cloned.1.call-start = ((), (), s32[]{:S(2)}) async-start(), calls=%async_computation.6 | async-start | bytes 2228224 | tf_op jit(solution)/shard_map/all_gather | solution.py:516
  13.8 293.4 %all-gather.17.cloned.1.call-start = ((), (), s32[]{:S(2)}) async-start(), calls=%async_computation.8 | async-start | bytes 6127616 | tf_op jit(solution)/shard_map/all_gather | solution.py:517
  14.6 346.6 %all-gather.15.cloned.1.call-start = ((), (), s32[]{:S(2)}) async-start(), calls=%async_computation.7 | async-start | bytes 6291456 | tf_op jit(solution)/shard_map/all_gather | solution.py:452
  72.2 87.2 %copy-start.11 = (f32[2048]{0:T(1024)}, f32[2048]{0:T(1024)S(1)}, u32[]{:S(2)}) copy-start(f32[2048]{0:T(1024)S(1)} %add_rsqrt_fusion) | copy-start | bytes 24580
  137.2 22.2 %copy-start.9 = (f32[1024]{0:T(1024)}, f32[1024]{0:T(1024)S(1)}, u32[]{:S(2)}) copy-start(f32[1024]{0:T(1024)S(1)} %get-tuple-element.89) | copy-start | bytes 12292
  238.5 2.0 copy-start
  240.5 2.0 copy-start.2
  248.4 48.1 %collective-permute-start = (bf16[1024,1024]{0,1:T(8,128)(2,1)}, bf16[1024,1024]{0,1:T(8,128)(2,1)}, u32[]{:S(2)}, u32[]{:S(2)}) collective-permute-start(bf16[1024,1024]{0,1:T(8,128)(2,1)} %fusion.33), channel_id=1, source_target_pairs={{0,1},{1,0},{2,3},{3,2},{4,5},{5,4},{6,7},{7,6},{8,9},{9,8},{10,11... | collective-permute-start | bytes 6291464 | tf_op jit(solution)/shard_map/ppermute | solution.py:467
  302.0 2.0 copy-start.3
  305.7 113.7 %all-gather.19.cloned.1.call-start = ((), (), s32[]{:S(2)}) async-start(), calls=%async_computation.9 | async-start | bytes 6291456 | tf_op jit(solution)/shard_map/all_gather | solution.py:452
  306.3 159.8 %all-gather.21.cloned.1.call-start = ((), (), s32[]{:S(2)}) async-start(), calls=%async_computation.10 | async-start | bytes 3063808 | tf_op jit(solution)/shard_map/all_gather | solution.py:520
  307.1 321.2 %all-gather.23.cloned.1.call-start = ((), (), s32[]{:S(2)}) async-start(), calls=%async_computation.11 | async-start | bytes 6291456 | tf_op jit(solution)/shard_map/all_gather | solution.py:452
  508.1 48.1 %collective-permute-start.1 = (bf16[1024,1024]{0,1:T(8,128)(2,1)}, bf16[1024,1024]{0,1:T(8,128)(2,1)}, u32[]{:S(2)}, u32[]{:S(2)}) collective-permute-start(bf16[1024,1024]{0,1:T(8,128)(2,1)} %fusion.36), channel_id=1, source_target_pairs={{0,1},{1,0},{2,3},{3,2},{4,5},{5,4},{6,7},{7,6},{8,9},{9,8},{10,11... | collective-permute-start | bytes 6291464 | tf_op jit(solution)/shard_map/ppermute | solution.py:467
  513.5 54.2 %copy-start.4 = (f32[1024,1024]{0,1:T(8,128)S(1)}, f32[1024,1024]{0,1:T(8,128)}, u32[]{:S(2)}) copy-start(f32[1024,1024]{0,1:T(8,128)} %copy-done.3) | copy-start | bytes 12582916
  513.5 54.3 %copy-start.5 = (bf16[1024,1024]{0,1:T(8,128)(2,1)S(1)}, bf16[1024,1024]{0,1:T(8,128)(2,1)}, u32[]{:S(2)}) copy-start(bf16[1024,1024]{0,1:T(8,128)(2,1)} %copy.101) | copy-start | bytes 6291460
  573.0 331.7 %reduce-scatter.11.cloned.1.call-start = ((), (), s32[]{:S(2)}) async-start(), calls=%async_computation.16 | async-start | bytes 3063808 | tf_op jit(solution)/shard_map/reduce_scatter | solution.py:475
  584.9 380.7 %all-reduce.7.cloned.1.call-start = ((), (), s32[]{:S(2)}) async-start(), calls=%async_computation.12 | async-start | bytes 155648 | tf_op jit(solution)/shard_map/psum | solution.py:572
  628.2 10.9 copy-start.1
  628.2 145.6 %slice-start = ((s8[6553600]{0:T(1024)(128)(4,1)}), s8[4194304]{0:T(1024)(128)(4,1)S(1)}, s32[]{:S(2)}) async-start(s8[6553600]{0:T(1024)(128)(4,1)} %bitcast.68), calls=%async_computation.17 | async-start | bytes 8388608
  639.1 134.7 %slice-start.1 = ((s8[6553600]{0:T(1024)(128)(4,1)}), s8[2359296]{0:T(1024)(128)(4,1)S(1)}, s32[]{:S(2)}) async-start(s8[6553600]{0:T(1024)(128)(4,1)} %bitcast.68), calls=%async_computation.18 | async-start | bytes 4718592
  773.9 58.0 %copy-start.10 = (f32[1024]{0:T(1024)S(1)}, f32[1024]{0:T(1024)}, u32[]{:S(2)}) copy-start(f32[1024]{0:T(1024)} %copy-done.9) | copy-start | bytes 12292
  784.3 47.7 %collective-permute-start.3 = (bf16[1024,1024]{0,1:T(8,128)(2,1)}, bf16[1024,1024]{0,1:T(8,128)(2,1)}, u32[]{:S(2)}, u32[]{:S(2)}) collective-permute-start(bf16[1024,1024]{0,1:T(8,128)(2,1)} %fusion.39), channel_id=1, source_target_pairs={{0,1},{1,0},{2,3},{3,2},{4,5},{5,4},{6,7},{7,6},{8,9},{9,8},{10,11... | collective-permute-start | bytes 6291464 | tf_op jit(solution)/shard_map/ppermute | solution.py:467
  846.3 207.3 %reduce-scatter.9.cloned.1.call-start = ((), (), s32[]{:S(2)}) async-start(), calls=%async_computation.15 | async-start | bytes 6127616 | tf_op jit(solution)/shard_map/reduce_scatter | solution.py:475
  865.6 9.4 copy-start.12
  865.6 252.8 %reduce-scatter.7.cloned.1.call-start = ((), (), s32[]{:S(2)}) async-start(), calls=%async_computation.14 | async-start | bytes 2228224 | tf_op jit(solution)/shard_map/reduce_scatter | solution.py:475
  874.9 333.4 %reduce-scatter.5.cloned.1.call-start = ((), (), s32[]{:S(2)}) async-start(), calls=%async_computation.13 | async-start | bytes 6963200 | tf_op jit(solution)/shard_map/reduce_scatter | solution.py:475
  904.3 47.0 %collective-permute-start.2 = (bf16[1024,1024]{0,1:T(8,128)(2,1)}, bf16[1024,1024]{0,1:T(8,128)(2,1)}, u32[]{:S(2)}, u32[]{:S(2)}) collective-permute-start(bf16[1024,1024]{0,1:T(8,128)(2,1)} %fusion.42), channel_id=1, source_target_pairs={{0,1},{1,0},{2,3},{3,2},{4,5},{5,4},{6,7},{7,6},{8,9},{9,8},{10,11... | collective-permute-start | bytes 6291464 | tf_op jit(solution)/shard_map/ppermute | solution.py:467
Sparse Core Ops, SparseCore 0:
  9.6 59.4 all-gather.8
  71.9 63.3 all-gather.10
  138.1 39.9 all-gather.12
  180.8 57.6 all-gather.16
  305.9 55.3 all-gather.14
  362.6 56.7 all-gather.18
  421.7 44.3 all-gather.20
  573.1 55.0 all-gather.22
  632.0 65.1 reduce-scatter.10
  846.5 119.1 all-reduce.6
  970.0 83.5 reduce-scatter.8
  1057.6 60.6 reduce-scatter.6
  1122.3 85.9 reduce-scatter.4

commit v2 on v1

--- a/solution.py
+++ b/solution.py
@@ -200,6 +200,9 @@
     states,
     solves,
     grads,
+    gate_up_part,
+    down_part,
+    out_part,
     d_mixed,
     d_conv,
     d_par,
@@ -395,7 +398,7 @@
     )(mixed, conv, par, head_gain)
 
 
-def core_backward(mixed, conv, par, head_gain, states, solves, grads, heads):
+def core_backward(mixed, conv, par, head_gain, states, solves, grads, heads, earlier_sums):
     count = mixed.shape[0]
     seqs, chunks = count // LEN, LEN // CHUNK
     width = 2 * DK + DV
@@ -416,7 +419,8 @@
             slab(heads * DK, DV),
             slab(heads * CHUNK, CHUNK),
             rows(heads * DV),
-        ],
+        ]
+        + [pl.BlockSpec(memory_space=pl.ANY)] * len(earlier_sums),
         out_specs=[
             rows(mixed.shape[1]),
             fixed(STEPS, conv.shape[1]),
@@ -439,7 +443,7 @@
             flops=count * heads * 900000, bytes_accessed=count * heads * 12000, transcendentals=0
         ),
         name="core_backward",
-    )(mixed, mixed, conv, par, head_gain, states, solves, grads)
+    )(mixed, mixed, conv, par, head_gain, states, solves, grads, *earlier_sums)
 
 
 def spread_lanes(pairs, lanes):
@@ -449,7 +453,17 @@
 
 
 def gather_rows(piece):
-    return lax.all_gather(piece, "tensor", axis=0, tiled=True)
+    size = lax.axis_size("tensor")
+    place = lax.axis_index("tensor")
+    rows = piece.shape[0]
+    whole = jnp.zeros((size * rows,) + piece.shape[1:], piece.dtype)
+    whole = lax.dynamic_update_slice_in_dim(whole, piece, place * rows, axis=0)
+    for shift in range(1, size):
+        pairs = [(source, (source + shift) % size) for source in range(size)]
+        arrived = lax.ppermute(piece, "tensor", pairs)
+        owner = (place + size - shift) % size
+        whole = lax.dynamic_update_slice_in_dim(whole, arrived, owner * rows, axis=0)
+    return whole
 
 
 def row_sums(rows, product):
@@ -473,8 +487,12 @@
 
 def scatter_sum(partial_value, axis):
     return lax.psum_scatter(
-        partial_value.astype(jnp.bfloat16), "dp", scatter_dimension=axis, tiled=True
+        partial_value, "dp", scatter_dimension=axis, tiled=True
     ).astype(jnp.float32)
+
+
+def row_gradient(left, right):
+    return contract_rows(left, right).astype(jnp.bfloat16)
 
 
 def per_device(
@@ -533,7 +551,8 @@
         axis=0,
     )
     gated, states, solves = core_forward(mixed, conv, par, head_scale, heads)
-    middle = residual + row_sums(gated, lambda rows: matmul(rows, out_matrix))
+    gathered = 0.0 * (back_rows[0, 0] + down_full[0, 0] + gate_up_matrix[0, 0]).astype(jnp.float32)
+    middle = (residual + gathered) + row_sums(gated, lambda rows: matmul(rows, out_matrix))
     piece_two = (rms_scale(middle) * mlp_scale).astype(jnp.bfloat16)
     normed_two = gather_rows(piece_two)
     both = matmul(normed_two, gate_up_matrix)
@@ -546,8 +565,10 @@
     d_up = d_hidden * gate * sigmoid_gate
     d_both = jnp.concatenate([d_gate, d_up], axis=1).astype(jnp.bfloat16)
     d_normed_two = row_sums(d_both, lambda rows: contract_last(rows, gate_up_matrix))
-    gate_up_sum = scatter_sum(contract_rows(normed_two, d_both), 0)
-    down_sum = scatter_sum(contract_rows(hidden, back_rows), 1)
+    gate_up_part = row_gradient(normed_two, d_both)
+    down_part = row_gradient(hidden, back_rows)
+    gate_up_sum = scatter_sum(gate_up_part, 0)
+    down_sum = scatter_sum(down_part, 1)
     d_middle, grad_mlp_gain = rms_back(middle, mlp_scale, d_normed_two)
     d_middle = d_middle + cotangent.astype(jnp.float32)
     middle_rows = gather_rows(d_middle.astype(jnp.bfloat16))
@@ -555,17 +576,22 @@
     block_output = (middle + row_sums(hidden_late, lambda rows: matmul(rows, down_full))).astype(
         jnp.bfloat16
     )
-    out_sum = scatter_sum(contract_rows(gated, middle_rows), 1)
+    out_part = row_gradient(gated, middle_rows)
+    out_sum = scatter_sum(out_part, 1)
     d_gated = contract_last(middle_rows, out_matrix)
     d_mixed, d_conv, d_par, d_head = core_backward(
-        mixed, conv, par, head_scale, states, solves, d_gated, heads
-    )
-    mix_sum = scatter_sum(contract_rows(normed_one, d_mixed), 0)
+        mixed, conv, par, head_scale, states, solves, d_gated, heads,
+        (gate_up_part, down_part, out_part),
+    )
+    summed = 0.0 * (gate_up_sum[0, 0] + down_sum[0, 0] + out_sum[0, 0])
+    mix_part = (contract_rows(normed_one, d_mixed) + summed).astype(jnp.bfloat16)
+    mix_sum = scatter_sum(mix_part, 0)
     d_normed_one = row_sums(d_mixed, lambda rows: contract_last(rows, mix_matrix))
     d_inputs, grad_attn_gain = rms_back(residual, attn_scale, d_normed_one)
     input_grad = (d_inputs + d_middle).astype(jnp.bfloat16)
 
     own = jnp.concatenate([d_conv[:CONV].reshape(-1), d_par[:2].reshape(-1)])
+    own = own + 0.0 * mix_part[0, 0].astype(jnp.float32)
     size = lax.axis_size("tensor")
     place = lax.axis_index("tensor")
     spread = jnp.where(jnp.arange(size)[:, None] == place, own[None], 0.0).reshape(-1)

time: 1220 us -> 960 us (0.79)
  waiting for transfers between devices: 706 us -> 434 us
  matrix products: 219 us -> 196 us
  local copies, waits for them, and re-layouts: 39.5 us -> 60.6 us
    all_gather x4 -> x0, waiting for transfers between devices: 189 us -> none  [gather_rows(): return lax.all_gather(piece, 'tensor', axis=0, tiled=True)]
    reduce_scatter x4 -> x2, waiting for transfers between devices: 233 us -> 87.4 us  [scatter_sum(): lax.psum_scatter(partial_value, 'dp', scatter_dimension=axis, tiled=True)]
    ppermute x0 -> x4, waiting for transfers between devices: none -> 132 us  [gather_rows(): arrived = lax.ppermute(piece, 'tensor', pairs)]
    all_gather x1, waiting for transfers between devices: 63.2 us -> 7.43 us  [per_device(): mix_matrix = lax.all_gather(packed, 'dp', axis=0, tiled=True)]
    psum x1, waiting for transfers between devices: 3.71 us -> 56.9 us  [per_device(): lax.psum(jnp.concatenate([grad_attn_gain, grad_mlp_gain, d_head[0], sprea...]
    all_gather x1, waiting for transfers between devices: 46.7 us -> 0.01 us  [per_device(): down_full = lax.all_gather(w_down, 'dp', axis=1, tiled=True)]
    ppermute x4, waiting for transfers between devices: 168 us -> 123 us  [row_sums(): arrived.append(lax.ppermute(sent, 'tensor', pairs))]
    all_gather x1, waiting for transfers between devices: 0.02 us -> 25.9 us  [per_device(): lax.all_gather(w_gate_up.reshape(slices, 2 * units), 'dp', axis=0, tiled=...]
  transfers between devices with their start and end apart: 17 -> 17, of which waited for: 14 -> 11; matrix products, arithmetic and copies ran while one was open for 17% -> 18% of each run, Pallas kernels for 18% -> 22%
where the time goes in v2:
time: 960 us; the launch traced here: 952 us
  waiting for transfers between devices  434 us (45%)
  Pallas kernels  214 us (22%)
  matrix products  196 us (20%)
  local copies, waits for them, and re-layouts  60.6 us (6%)
  between operations  19.4 us (2%)
  other arithmetic  14.7 us (2%)
  starting transfers between devices  12.3 us (1%)
    pallas_call x1, Pallas kernels, core_backward(): pl.pallas_call(functools.partial(backward_kernel, heads), grid=(seqs, chu...  135 us
    ppermute x4, waiting for transfers between devices, gather_rows(): arrived = lax.ppermute(piece, 'tensor', pairs)  132 us
    ppermute x4, waiting for transfers between devices, row_sums(): arrived.append(lax.ppermute(sent, 'tensor', pairs))  123 us
    reduce_scatter x2, waiting for transfers between devices, scatter_sum(): lax.psum_scatter(partial_value, 'dp', scatter_dimension=axis, tiled=True)  87.4 us
    dot_general x6, matrix products, contract_last(): lax.dot_general(left, right, (((1,), (1,)), ((), ())), preferred_element_...  80.1 us
    pallas_call x1, Pallas kernels, core_forward(): pl.pallas_call(functools.partial(forward_kernel, heads), grid=(seqs, chun...  79.3 us
    dot_general x6, matrix products, matmul(): return jnp.dot(left, right, preferred_element_type=jnp.float32)  63 us
    psum x1, waiting for transfers between devices, per_device(): lax.psum(jnp.concatenate([grad_attn_gain, grad_mlp_gain, d_head[0], sprea...  56.9 us
  transfers between devices with their start and end apart: 17, of which 11 were waited for; matrix products, arithmetic and copies ran while one was open for 18% of the time, Pallas kernels for 22%

profile of v2, /device:TPU:0, one launch (start us, length us, event | category | flops | bytes accessed | tf_op | source)
XLA Modules:
  0.0 951.5 jit_solution(5382993599372638637)
XLA Ops:
  7.2 1.2 copy.89
  12.4 1.6 copy.87
  14.8 1.8 copy.88
  16.6 3.0 collective-permute-start.1
  23.2 43.2 %collective-permute-done.1 = bf16[1024,1024]{1,0:T(8,128)(2,1)} collective-permute-done((bf16[1024,1024]{1,0:T(8,128)(2,1)}, bf16[1024,1024]{1,0:T(8,128)(2,1)}, u32[]{:S(2)}, u32[]{:S(2)}) %collective-permute-start.1) | collective-permute-done | bytes 2097184 | tf_op jit(solution)/shard_map/ppermute | solution.py:463
  66.5 1.9 constant_dynamic-update-slice_fusion.4
  68.4 1.9 copy-done.12
  71.2 7.4 all-gather.9.cloned.1.call-done
  78.6 1.1 slice_convert_fusion
  80.7 22.0 %fusion.51.mixed.before = f32[2048,3200]{1,0:T(8,128)} fusion(bf16[1024,3200]{1,0:T(8,128)(2,1)} %all-gather.9.cloned.1.call-done, bf16[2048,1024]{1,0:T(8,128)(2,1)} %copy-done.12, f32[1024]{0:T(1024)S(1)} %get-tuple-element.89, f32[2048]{0:T(1024)S(1)} %add_rsqrt_fusion), kind=kOutput, calls=%fused_computation.61 | convolution fusion | flops 13430161408 | bytes 36974592 | tf_op jit(solution)/shard_map/dot_general | solution.py:37
  102.7 79.3 %core_forward.1 = (bf16[2048,1024]{1,0:T(8,128)(2,1)S(1)}, f32[16,512,256]{2,1,0:T(8,128)}, f32[16,512,128]{2,1,0:T(8,128)S(1)}) custom-call(f32[2048,3200]{1,0:T(8,128)} %fusion.51.mixed.before, f32[4,2048]{1,0:T(4,128)S(1)} %bitcast.60, f32[8,128]{1,0:T(8,128)S(1)} %fusion.61.par, f32[1,256]{1,0:T(1,128)S(1)} %reshape.155.head_gain), custom_call_target="tpu_custom_call" | custom-call | flops 4915200000 | bytes 81920000 | tf_op jit(solution)/shard_map/core_forward/pallas_call | solution.py:374
  182.0 2.0 copy-done.1
  184.0 2.0 copy-done.8
  186.0 5.9 fusion.34
  192.0 1.5 collective-permute-start.2
  194.3 1.9 constant_dynamic-update-slice_fusion.6
  196.1 2.1 copy-done.20
  198.8 1.1 slice.124
  201.2 25.9 %all-gather.7.cloned.1.call-done = bf16[1024,2816]{1,0:T(8,128)(2,1)} async-done(((bf16[64,2816]{1,0:T(8,128)(2,1)}), bf16[1024,2816]{1,0:T(8,128)(2,1)}) %all-gather.7.cloned.1.call-update) | async-done | bytes 5767184 | tf_op jit(solution)/shard_map/all_gather | solution.py:535
  227.2 1.2 slice.125
  229.0 11.0 %collective-permute-done.2 = bf16[1024,1024]{1,0:T(8,128)(2,1)} collective-permute-done((bf16[1024,1024]{1,0:T(8,128)(2,1)}, bf16[1024,1024]{1,0:T(8,128)(2,1)}, u32[]{:S(2)}, u32[]{:S(2)}) %collective-permute-start.2) | collective-permute-done | bytes 2097184 | tf_op jit(solution)/shard_map/ppermute | solution.py:481
  240.1 5.6 multiply_reduce_fusion.2
  246.7 1.1 copy-done.13
  247.8 1.5 collective-permute-start.3
  249.3 45.5 %collective-permute-done.3 = bf16[1024,1024]{1,0:T(8,128)(2,1)S(1)} collective-permute-done((bf16[1024,1024]{1,0:T(8,128)(2,1)S(1)}, bf16[1024,1024]{1,0:T(8,128)(2,1)S(1)}, u32[]{:S(2)}, u32[]{:S(2)}) %collective-permute-start.3) | collective-permute-done | bytes 2097184 | tf_op jit(solution)/shard_map/ppermute | solution.py:463
  295.1 1.9 copy-done.19
  297.0 15.2 %fusion.67 = f32[2048,2816]{1,0:T(8,128)} fusion(bf16[2048,1024]{1,0:T(8,128)(2,1)S(1)} %constant_dynamic-update-slice_fusion.2, bf16[1024,2816]{1,0:T(8,128)(2,1)S(1)} %bitcast.85), kind=kOutput, calls=%fused_computation.108 | convolution fusion | flops 11811160064 | bytes 33030144 | tf_op jit(solution)/shard_map/dot_general | solution.py:37
  312.2 21.5 %multiply_convert_fusion = (bf16[2048,1408]{1,0:T(8,128)(2,1)}, bf16[2048,1408]{1,0:T(8,128)(2,1)}, bf16[2048,1408]{1,0:T(8,128)(2,1)}) fusion(f32[2048,2816]{1,0:T(8,128)} %fusion.67, bf16[2048,1024]{1,0:T(8,128)(2,1)} %copy-done.20, bf16[1408,1024]{0,1:T(8,128)(2,1)S(1)} %copy-done.27), kind=kOutput, calls=%fused_computation.7 | convolution fusion | flops 5951717376 | bytes 47448064 | tf_op jit(solution)/shard_map/dot_general | solution.py:47
  333.7 11.0 %fusion.37 = bf16[1024,1024]{1,0:T(8,128)(2,1)} fusion(bf16[1024,2816]{1,0:T(8,128)(2,1)} %all-gather.7.cloned.1.call-done, s32[]{:T(128)S(6)} %select_n.61, bf16[2048,1408]{1,0:T(8,128)(2,1)} %get-tuple-element.96, bf16[2048,1408]{1,0:T(8,128)(2,1)} %get-tuple-element.95), kind=kOutput, calls=%fused_computation.57 | convolution fusion | flops 5918162944 | bytes 19398660 | tf_op jit(solution)/shard_map/dot_general | solution.py:47
  344.7 1.5 collective-permute-start.4
  346.1 6.5 convolution_convert_fusion.down_part
  352.7 2.9 copy.80
  355.6 35.4 %collective-permute-done.4 = bf16[1024,1024]{1,0:T(8,128)(2,1)} collective-permute-done((bf16[1024,1024]{1,0:T(8,128)(2,1)}, bf16[1024,1024]{1,0:T(8,128)(2,1)}, u32[]{:S(2)}, u32[]{:S(2)}) %collective-permute-start.4) | collective-permute-done | bytes 2097184 | tf_op jit(solution)/shard_map/ppermute | solution.py:481
  391.0 12.3 %multiply_reduce_fusion = (f32[1024]{0:T(1024)S(1)}, f32[1024]{0:T(1024)S(1)}, f32[1024,1024]{1,0:T(8,128)S(1)}) fusion(f32[1024,1024]{1,0:T(8,128)} %copy-done.13, f32[1024]{0:T(1024)S(1)} %add_rsqrt_fusion.2, bf16[1024,1024]{1,0:T(8,128)(2,1)} %collective-permute-done.4, f32[1024]{0:T(1024)S(1)} %get-tuple-element.87, ...), kind=kOutput, calls=%fused_computation.39 | convolution fusion | flops 5925500928 | bytes 27803652 | tf_op jit(solution)/shard_map/dot_general | solution.py:47
  403.9 1.7 copy-done.14
  405.6 4.3 constant_dynamic-update-slice_fusion.1
  409.9 1.4 collective-permute-start.5
  411.3 43.6 %collective-permute-done.5 = bf16[1024,1024]{1,0:T(8,128)(2,1)S(1)} collective-permute-done((bf16[1024,1024]{1,0:T(8,128)(2,1)S(1)}, bf16[1024,1024]{1,0:T(8,128)(2,1)S(1)}, u32[]{:S(2)}, u32[]{:S(2)}) %collective-permute-start.5) | collective-permute-done | bytes 2097184 | tf_op jit(solution)/shard_map/ppermute | solution.py:463
  455.1 2.1 copy-done.18
  457.2 5.8 convolution_convert_fusion.1.out_part
  463.0 3.9 copy.82
  467.0 19.2 %fusion.17.gate_up_part = bf16[1024,2816]{1,0:T(8,128)(2,1)} fusion(bf16[2048,1024]{1,0:T(8,128)(2,1)} %copy-done.19, bf16[2048,1408]{1,0:T(8,128)(2,1)} %get-tuple-element.95, bf16[2048,1408]{1,0:T(8,128)(2,1)} %get-tuple-element.96), kind=kOutput, calls=%fused_computation.30 | convolution fusion | flops 11837112320 | bytes 21495808 | tf_op jit(solution)/shard_map/dot_general | solution.py:41
  486.3 10.9 %fusion.68.grads = f32[2048,1024]{1,0:T(8,128)} fusion(bf16[2048,1024]{1,0:T(8,128)(2,1)} %copy-done.18, bf16[1024,1024]{0,1:T(8,128)(2,1)} %all-gather.11.cloned.1.call-done), kind=kOutput, calls=%fused_computation.109 | convolution fusion | flops 4294967296 | bytes 14680064 | tf_op jit(solution)/shard_map/dot_general | solution.py:47
  497.2 134.7 %core_backward.1 = (bf16[2048,3200]{1,0:T(8,128)(2,1)}, f32[8,2048]{1,0:T(8,128)S(1)}, f32[8,128]{1,0:T(8,128)S(1)}, f32[8,256]{1,0:T(8,128)S(1)}) custom-call(f32[2048,3200]{1,0:T(8,128)} %fusion.51.mixed.before, f32[2048,3200]{1,0:T(8,128)} %fusion.51.mixed.before, f32[4,2048]{1,0:T(4,128)S(1)} %bitcast.61, f32[8,128]{1,0:T(8,128)S(1)} %copy-done.5, ...), custom_call_target="tpu_custom_call" | custom-call | flops 7372800000 | bytes 98304000 | tf_op jit(solution)/shard_map/core_backward/pallas_call | solution.py:410
  631.9 10.5 %fusion.40 = bf16[1024,1024]{1,0:T(8,128)(2,1)} fusion(bf16[1024,3200]{1,0:T(8,128)(2,1)S(1)} %bitcast.77, bf16[2048,3200]{1,0:T(8,128)(2,1)} %get-tuple-element.27, s32[]{:T(128)S(6)} %select_n.61), kind=kOutput, calls=%fused_computation.58 | convolution fusion | flops 6711934976 | bytes 15204356 | tf_op jit(solution)/shard_map/dot_general | solution.py:47
  642.5 1.5 collective-permute-start.7
  644.5 1.1 copy.81
  646.2 40.6 %collective-permute-done.7 = bf16[1024,1024]{1,0:T(8,128)(2,1)} collective-permute-done((bf16[1024,1024]{1,0:T(8,128)(2,1)}, bf16[1024,1024]{1,0:T(8,128)(2,1)}, u32[]{:S(2)}, u32[]{:S(2)}) %collective-permute-start.7) | collective-permute-done | bytes 2097184 | tf_op jit(solution)/shard_map/ppermute | solution.py:481
  686.8 14.0 %fusion.23 = (f32[1024]{0:T(1024)S(1)}, f32[1024]{0:T(1024)S(1)}, f32[1024,1024]{1,0:T(8,128)}) fusion(bf16[1024,1024]{1,0:T(8,128)(2,1)S(1)} %copy-done.11, f32[1024]{0:T(1024)S(1)} %add_rsqrt_fusion.1, bf16[1024,1024]{1,0:T(8,128)(2,1)} %collective-permute-done.7, f32[1024]{0:T(1024)S(1)} %copy-done.24, ...), kind=kOutput, calls=%fused_computation.36 | convolution fusion | flops 6720321536 | bytes 21512196 | tf_op jit(solution)/shard_map/dot_general | solution.py:47
  700.8 1.1 copy.83
  702.4 1.2 slice.133
  705.6 21.6 %add_convert_fusion = bf16[1024,3200]{1,0:T(8,128)(2,1)} fusion(bf16[2048,3200]{1,0:T(8,128)(2,1)} %get-tuple-element.27, f32[]{:T(128)} %bitcast.9, bf16[2048,1024]{1,0:T(8,128)(2,1)} %copy-done.12, f32[1024]{0:T(1024)S(1)} %copy-done.24, f32[2048]{0:T(1024)S(1)} %copy-done.26), kind=kOutput, calls=%fused_computation.5 | convolution fusion | flops 13436715008 | bytes 23867396 | tf_op jit(solution)/shard_map/dot_general | solution.py:41
  727.2 1.1 slice.136
  730.6 7.5 fusion.43
  738.0 1.6 collective-permute-start.6
  739.6 0.9 copy.77
  740.5 5.9 fusion.22
  746.4 35.6 %collective-permute-done.6 = bf16[1024,1024]{1,0:T(8,128)(2,1)} collective-permute-done((bf16[1024,1024]{1,0:T(8,128)(2,1)}, bf16[1024,1024]{1,0:T(8,128)(2,1)}, u32[]{:S(2)}, u32[]{:S(2)}) %collective-permute-start.6) | collective-permute-done | bytes 2097184 | tf_op jit(solution)/shard_map/ppermute | solution.py:481
  782.0 6.8 add_convert_fusion.1
  789.8 1.3 reshape.161
  791.1 56.9 %all-reduce.7.cloned.1.call-done = f32[19200]{0:T(1024)} async-done(((f32[19200]{0:T(1024)}), f32[19200]{0:T(1024)}) %all-reduce.7.cloned.1.call-update) | async-done | bytes 76816 | tf_op jit(solution)/shard_map/psum | solution.py:598
  853.4 87.4 %reduce-scatter.11.cloned.1.call-done = bf16[64,3200]{1,0:T(8,128)(2,1)} async-done(((bf16[1024,3200]{1,0:T(8,128)(2,1)}), bf16[64,3200]{1,0:T(8,128)(2,1)}) %reduce-scatter.11.cloned.1.call-update) | async-done | bytes 409616 | tf_op jit(solution)/shard_map/reduce_scatter | solution.py:489
  940.9 1.0 slice.138
  941.9 1.3 reshape.157
  (151 shorter events, 24.7 us)
Async XLA Ops:
  7.2 15.7 %copy-start.10 = (bf16[1024,1024]{1,0:T(8,128)(2,1)S(1)}, bf16[1024,1024]{1,0:T(8,128)(2,1)}, u32[]{:S(2)}) copy-start(bf16[1024,1024]{1,0:T(8,128)(2,1)} %param.13) | copy-start | bytes 6291460
  7.2 71.5 %all-gather.9.cloned.1.call-start = ((), (), s32[]{:S(2)}) async-start(), calls=%async_computation.6 | async-start | bytes 6963200 | tf_op jit(solution)/shard_map/all_gather | solution.py:529
  12.4 173.6 %all-gather.11.cloned.1.call-start = ((), (), s32[]{:S(2)}) async-start(), calls=%async_computation.7 | async-start | bytes 2228224 | tf_op jit(solution)/shard_map/all_gather | solution.py:534
  14.0 184.7 %all-gather.5.cloned.1.call-start = ((), (), s32[]{:S(2)}) async-start(), calls=%async_computation.4 | async-start | bytes 3063808 | tf_op jit(solution)/shard_map/all_gather | solution.py:538
  14.8 212.4 %all-gather.7.cloned.1.call-start = ((), (), s32[]{:S(2)}) async-start(), calls=%async_computation.5 | async-start | bytes 6127616 | tf_op jit(solution)/shard_map/all_gather | solution.py:535
  16.6 627.9 %reduce-scatter.13.cloned.1.call-start = ((), (), s32[]{:S(2)}) async-start(), calls=%async_computation.11 | async-start | bytes 3063808
  16.6 49.8 %collective-permute-start.1 = (bf16[1024,1024]{1,0:T(8,128)(2,1)}, bf16[1024,1024]{1,0:T(8,128)(2,1)}, u32[]{:S(2)}, u32[]{:S(2)}) collective-permute-start(bf16[1024,1024]{1,0:T(8,128)(2,1)} %param.13), channel_id=1, source_target_pairs={{0,1},{1,0},{2,3},{3,2},{4,5},{5,4},{6,7},{7,6},{8,9},{9,8},{10,11... | collective-permute-start | bytes 6291464 | tf_op jit(solution)/shard_map/ppermute | solution.py:463
  19.7 174.6 %collective-permute-start = (bf16[1024,1024]{1,0:T(8,128)(2,1)}, bf16[1024,1024]{1,0:T(8,128)(2,1)}, u32[]{:S(2)}, u32[]{:S(2)}) collective-permute-start(bf16[1024,1024]{1,0:T(8,128)(2,1)} %param.25), channel_id=1, source_target_pairs={{0,1},{1,0},{2,3},{3,2},{4,5},{5,4},{6,7},{7,6},{8,9},{9,8},{10,11... | collective-permute-start | bytes 6291464 | tf_op jit(solution)/shard_map/ppermute | solution.py:463
  20.5 82.1 %copy-start.2 = (f32[1,4,4,512]{3,1,2,0:T(4,128)}, f32[1,4,4,512]{3,1,2,0:T(4,128)S(1)}, u32[]{:S(2)}) copy-start(f32[1,4,4,512]{3,1,2,0:T(4,128)S(1)} %copy.90) | copy-start | bytes 98308
  23.2 79.4 %copy-start.4 = (f32[8,128]{1,0:T(8,128)}, f32[8,128]{1,0:T(8,128)S(1)}, u32[]{:S(2)}) copy-start(f32[8,128]{1,0:T(8,128)S(1)} %fusion.61.par) | copy-start | bytes 12292
  68.3 1.9 copy-start.12
  71.2 31.5 %copy-start.25 = (f32[2048]{0:T(1024)}, f32[2048]{0:T(1024)S(1)}, u32[]{:S(2)}) copy-start(f32[2048]{0:T(1024)S(1)} %add_rsqrt_fusion) | copy-start | bytes 24580
  80.5 22.2 %copy-start.23 = (f32[1024]{0:T(1024)}, f32[1024]{0:T(1024)S(1)}, u32[]{:S(2)}) copy-start(f32[1024]{0:T(1024)S(1)} %get-tuple-element.89) | copy-start | bytes 12292
  80.7 22.0 %copy-start.6 = (f32[1,256]{1,0:T(1,128)}, f32[1,256]{1,0:T(1,128)S(1)}, u32[]{:S(2)}) copy-start(f32[1,256]{1,0:T(1,128)S(1)} %reshape.155.head_gain) | copy-start | bytes 3076
  182.0 2.0 copy-start.1
  184.0 2.0 copy-start.8
  192.0 2.0 copy-start.16
  192.0 48.1 %collective-permute-start.2 = (bf16[1024,1024]{1,0:T(8,128)(2,1)}, bf16[1024,1024]{1,0:T(8,128)(2,1)}, u32[]{:S(2)}, u32[]{:S(2)}) collective-permute-start(bf16[1024,1024]{1,0:T(8,128)(2,1)} %fusion.34), channel_id=1, source_target_pairs={{0,1},{1,0},{2,3},{3,2},{4,5},{5,4},{6,7},{7,6},{8,9},{9,8},{10,11... | collective-permute-start | bytes 6291464 | tf_op jit(solution)/shard_map/ppermute | solution.py:481
  196.1 2.1 copy-start.20
  245.6 2.1 copy-start.13
  245.7 51.3 %slice-start.2 = ((s8[5767168]{0:T(1024)(128)(4,1)}), s8[4194304]{0:T(1024)(128)(4,1)S(1)}, s32[]{:S(2)}) async-start(s8[5767168]{0:T(1024)(128)(4,1)} %bitcast.84), calls=%async_computation.15 | async-start | bytes 8388608
  246.2 50.8 %slice-start.3 = ((s8[5767168]{0:T(1024)(128)(4,1)}), s8[1572864]{0:T(1024)(128)(4,1)S(1)}, s32[]{:S(2)}) async-start(s8[5767168]{0:T(1024)(128)(4,1)} %bitcast.84), calls=%async_computation.16 | async-start | bytes 3145728
  247.8 47.0 %collective-permute-start.3 = (bf16[1024,1024]{1,0:T(8,128)(2,1)S(1)}, bf16[1024,1024]{1,0:T(8,128)(2,1)S(1)}, u32[]{:S(2)}, u32[]{:S(2)}) collective-permute-start(bf16[1024,1024]{1,0:T(8,128)(2,1)S(1)} %get-tuple-element.94), channel_id=1, source_target_pairs={{0,1},{1,0},{2,3},{3,2},{4,5},{5,4},{6,7},{7,6},{8,9},{9,8},{10,11... | collective-permute-start | bytes 6291464 | tf_op jit(solution)/shard_map/ppermute | solution.py:463
  295.0 1.9 copy-start.19
  297.0 15.2 %copy-start.27 = (bf16[1408,1024]{0,1:T(8,128)(2,1)S(1)}, bf16[1408,1024]{0,1:T(8,128)(2,1)}, u32[]{:S(2)}) copy-start(bf16[1408,1024]{0,1:T(8,128)(2,1)} %all-gather.5.cloned.1.call-done) | copy-start | bytes 8650756
  333.7 12.5 %copy-start.21 = (bf16[2048,1024]{1,0:T(8,128)(2,1)S(1)}, bf16[2048,1024]{1,0:T(8,128)(2,1)}, u32[]{:S(2)}) copy-start(bf16[2048,1024]{1,0:T(8,128)(2,1)} %copy-done.20) | copy-start | bytes 12582916
  333.7 12.5 %copy-start.29 = (bf16[2048,1408]{1,0:T(8,128)(2,1)S(1)}, bf16[2048,1408]{1,0:T(8,128)(2,1)}, u32[]{:S(2)}) copy-start(bf16[2048,1408]{1,0:T(8,128)(2,1)} %get-tuple-element.23) | copy-start | bytes 17301508
  344.7 46.4 %collective-permute-start.4 = (bf16[1024,1024]{1,0:T(8,128)(2,1)}, bf16[1024,1024]{1,0:T(8,128)(2,1)}, u32[]{:S(2)}, u32[]{:S(2)}) collective-permute-start(bf16[1024,1024]{1,0:T(8,128)(2,1)} %fusion.37), channel_id=1, source_target_pairs={{0,1},{1,0},{2,3},{3,2},{4,5},{5,4},{6,7},{7,6},{8,9},{9,8},{10,11... | collective-permute-start | bytes 6291464 | tf_op jit(solution)/shard_map/ppermute | solution.py:481
  355.6 345.2 %reduce-scatter.15.cloned.1.call-start = ((), (), s32[]{:S(2)}) async-start(), calls=%async_computation.12 | async-start | bytes 2228224
  391.0 12.8 %copy-start.17 = (bf16[1024,1024]{1,0:T(8,128)(2,1)S(1)}, bf16[1024,1024]{1,0:T(8,128)(2,1)}, u32[]{:S(2)}) copy-start(bf16[1024,1024]{1,0:T(8,128)(2,1)} %param.25) | copy-start | bytes 6291460
  403.3 2.3 copy-start.14
  409.9 47.3 %copy-start.9 = (bf16[2048,1024]{1,0:T(8,128)(2,1)S(1)}, bf16[2048,1024]{1,0:T(8,128)(2,1)}, u32[]{:S(2)}) copy-start(bf16[2048,1024]{1,0:T(8,128)(2,1)} %copy-done.8) | copy-start | bytes 12582916
  409.9 45.0 %collective-permute-start.5 = (bf16[1024,1024]{1,0:T(8,128)(2,1)S(1)}, bf16[1024,1024]{1,0:T(8,128)(2,1)S(1)}, u32[]{:S(2)}, u32[]{:S(2)}) collective-permute-start(bf16[1024,1024]{1,0:T(8,128)(2,1)S(1)} %get-tuple-element.91), channel_id=1, source_target_pairs={{0,1},{1,0},{2,3},{3,2},{4,5},{5,4},{6,7},{7,6},{8,9},{9,8},{10,11... | collective-permute-start | bytes 6291464 | tf_op jit(solution)/shard_map/ppermute | solution.py:463
  455.1 2.1 copy-start.18
  466.9 235.5 %reduce-scatter.9.cloned.1.call-start = ((), (), s32[]{:S(2)}) async-start(), calls=%async_computation.8 | async-start | bytes 6127616 | tf_op jit(solution)/shard_map/reduce_scatter | solution.py:489
  486.2 11.0 %copy-start.3 = (f32[1,4,4,512]{3,1,2,0:T(4,128)S(1)}, f32[1,4,4,512]{3,1,2,0:T(4,128)}, u32[]{:S(2)}) copy-start(f32[1,4,4,512]{3,1,2,0:T(4,128)} %copy-done.2) | copy-start | bytes 98308
  486.2 11.0 %copy-start.5 = (f32[8,128]{1,0:T(8,128)S(1)}, f32[8,128]{1,0:T(8,128)}, u32[]{:S(2)}) copy-start(f32[8,128]{1,0:T(8,128)} %copy-done.4) | copy-start | bytes 12292
  486.3 11.0 %copy-start.7 = (f32[1,256]{1,0:T(1,128)S(1)}, f32[1,256]{1,0:T(1,128)}, u32[]{:S(2)}) copy-start(f32[1,256]{1,0:T(1,128)} %copy-done.6) | copy-start | bytes 3076
  486.3 361.7 %all-reduce.7.cloned.1.call-start = ((), (), s32[]{:S(2)}) async-start(), calls=%async_computation.9 | async-start | bytes 155648 | tf_op jit(solution)/shard_map/psum | solution.py:598
  486.3 10.9 %copy-start = (bf16[1024,1024]{1,0:T(8,128)(2,1)S(1)}, bf16[1024,1024]{1,0:T(8,128)(2,1)}, u32[]{:S(2)}) copy-start(bf16[1024,1024]{1,0:T(8,128)(2,1)} %convolution_convert_fusion.1.out_part) | copy-start | bytes 6291460
  486.3 145.6 %slice-start = ((s8[6553600]{0:T(1024)(128)(4,1)}), s8[4194304]{0:T(1024)(128)(4,1)S(1)}, s32[]{:S(2)}) async-start(s8[6553600]{0:T(1024)(128)(4,1)} %bitcast.76), calls=%async_computation.13 | async-start | bytes 8388608
  497.2 134.7 %slice-start.1 = ((s8[6553600]{0:T(1024)(128)(4,1)}), s8[2359296]{0:T(1024)(128)(4,1)S(1)}, s32[]{:S(2)}) async-start(s8[6553600]{0:T(1024)(128)(4,1)} %bitcast.76), calls=%async_computation.14 | async-start | bytes 4718592
  631.9 12.0 %copy-start.11 = (bf16[1024,1024]{1,0:T(8,128)(2,1)S(1)}, bf16[1024,1024]{1,0:T(8,128)(2,1)}, u32[]{:S(2)}) copy-start(bf16[1024,1024]{1,0:T(8,128)(2,1)} %param.13) | copy-start | bytes 6291460
  631.9 54.9 %copy-start.24 = (f32[1024]{0:T(1024)S(1)}, f32[1024]{0:T(1024)}, u32[]{:S(2)}) copy-start(f32[1024]{0:T(1024)} %copy-done.23) | copy-start | bytes 12292
  642.5 44.4 %collective-permute-start.7 = (bf16[1024,1024]{1,0:T(8,128)(2,1)}, bf16[1024,1024]{1,0:T(8,128)(2,1)}, u32[]{:S(2)}, u32[]{:S(2)}) collective-permute-start(bf16[1024,1024]{1,0:T(8,128)(2,1)} %fusion.40), channel_id=1, source_target_pairs={{0,1},{1,0},{2,3},{3,2},{4,5},{5,4},{6,7},{7,6},{8,9},{9,8},{10,11... | collective-permute-start | bytes 6291464 | tf_op jit(solution)/shard_map/ppermute | solution.py:481
  646.2 59.4 %copy-start.26 = (f32[2048]{0:T(1024)S(1)}, f32[2048]{0:T(1024)}, u32[]{:S(2)}) copy-start(f32[2048]{0:T(1024)} %copy-done.25) | copy-start | bytes 24580
  729.8 211.0 %reduce-scatter.11.cloned.1.call-start = ((), (), s32[]{:S(2)}) async-start(), calls=%async_computation.10 | async-start | bytes 6963200 | tf_op jit(solution)/shard_map/reduce_scatter | solution.py:489
  738.0 44.0 %collective-permute-start.6 = (bf16[1024,1024]{1,0:T(8,128)(2,1)}, bf16[1024,1024]{1,0:T(8,128)(2,1)}, u32[]{:S(2)}, u32[]{:S(2)}) collective-permute-start(bf16[1024,1024]{1,0:T(8,128)(2,1)} %fusion.43), channel_id=1, source_target_pairs={{0,1},{1,0},{2,3},{3,2},{4,5},{5,4},{6,7},{7,6},{8,9},{9,8},{10,11... | collective-permute-start | bytes 6291464 | tf_op jit(solution)/shard_map/ppermute | solution.py:481
  740.5 41.6 %copy-start.15 = (f32[1024,1024]{1,0:T(8,128)S(1)}, f32[1024,1024]{1,0:T(8,128)}, u32[]{:S(2)}) copy-start(f32[1024,1024]{1,0:T(8,128)} %copy-done.13) | copy-start | bytes 12582916
  740.5 41.6 %copy-start.28 = (bf16[1408,1024]{0,1:T(8,128)(2,1)S(1)}, bf16[1408,1024]{0,1:T(8,128)(2,1)}, u32[]{:S(2)}) copy-start(bf16[1408,1024]{0,1:T(8,128)(2,1)} %all-gather.5.cloned.1.call-done) | copy-start | bytes 8650756
  746.4 43.4 %copy-start.22 = (bf16[64,2816]{1,0:T(8,128)(2,1)S(1)}, bf16[64,2816]{1,0:T(8,128)(2,1)}, u32[]{:S(2)}) copy-start(bf16[64,2816]{1,0:T(8,128)(2,1)} %reduce-scatter.9.cloned.1.call-done) | copy-start | bytes 1081348
Sparse Core Ops, SparseCore 0:
  12.5 66.0 all-gather.8
  81.4 39.9 all-gather.10
  123.6 43.2 all-gather.4
  169.7 57.4 all-gather.6
  355.7 62.8 reduce-scatter.12
  467.1 60.0 reduce-scatter.14
  531.1 80.5 reduce-scatter.8
  730.0 118.0 all-reduce.6
  852.0 88.8 reduce-scatter.10
